TPU v7x, 512 devices: a whole 4x4x16 slice. The times are simulated.
512 devices in a mesh: rows: 64 (over y, z), dims: 8 (over x, core).
Axes of the slice: x: 4, y: 4, z: 16, core: 2. Of those that a mesh axis runs over, the one named last changes fastest.
Arguments:
- vectors: bfloat16 [262144, 1024], P('rows', 'dims'), may hold values from -16 to 16
- list_ids: int32 [262144], P('rows'), may hold values from 0 to 65535, as said below
- codes: int32 [262144, 64], P('rows', 'dims'), may hold values from 0 to 255
- old_centroids: float32 [65536, 1024], P('rows', 'dims'), may hold values from -6 to 6
- old_codebooks: float32 [256, 1024], P('rows', 'dims'), may hold values from -6 to 6
Outputs:
- new_centroids: float32 [65536, 1024], P('rows', 'dims')
- list_error: float32 [65536], P('rows')
- new_codebooks: float32 [256, 1024], P('rows', 'dims')
Inputs may be any that keep to these rules, and one draw needn't show every extreme that they name: `list_ids`: among the vectors of one device, at most 128 name lists of any one aligned block of 1024 lists, and that bound is reached.
All inputs are finite; a program needn't handle non-finite values.
Results may differ from a plain program's by a relative error of at most 0.0003.
Values may be sent and summed in bfloat16 or wider, within the bound.
A program may use at most 64 MiB of HBM per device.

v0:
```python
import math

import jax
import jax.numpy as jnp
from jax import lax
from jax.sharding import PartitionSpec as P


def pack_rows(vectors, list_ids, codes, owner_count, owned):
    row_count, slice_width = vectors.shape
    capacity = 2 * row_count // owner_count
    owner_index = list_ids // owned
    owner_hits = (owner_index[:, None] == jnp.arange(owner_count, dtype=jnp.int32)[None, :]).astype(
        jnp.int32
    )
    rank_index = jnp.sum(jnp.cumsum(owner_hits, axis=0) * owner_hits, axis=1) - 1
    slot_index = owner_index * capacity + rank_index
    slot_total = owner_count * capacity
    send_vec = jnp.zeros((slot_total, slice_width), vectors.dtype).at[slot_index].set(vectors)
    send_ids = jnp.full((slot_total,), -1, jnp.int32).at[slot_index].set(list_ids)
    send_codes = jnp.full((slot_total, codes.shape[1]), -1, jnp.int32).at[slot_index].set(codes)
    return (
        slot_index,
        send_vec.reshape(owner_count, capacity, slice_width),
        send_ids.reshape(owner_count, capacity),
        send_codes.reshape(owner_count, capacity, codes.shape[1]),
    )


def refit_lists(recv_vec, recv_ids, old_centroids, first_list):
    slice_width = recv_vec.shape[-1]
    received = recv_vec.reshape(-1, slice_width)
    flat_ids = recv_ids.reshape(-1)
    local_index = flat_ids - first_list
    owned = old_centroids.shape[0]
    block_size = math.gcd(owned, 256)

    def per_block(list_start):
        wanted = list_start + jnp.arange(block_size, dtype=jnp.int32)
        matches = wanted[:, None] == local_index[None, :]
        totals = jnp.dot(matches.astype(jnp.bfloat16), received, preferred_element_type=jnp.float32)
        counts = jnp.sum(matches, axis=1).astype(jnp.float32)
        return (totals, counts)

    starts = jnp.arange(owned // block_size, dtype=jnp.int32) * block_size
    totals, counts = lax.map(per_block, starts)
    totals = totals.reshape(owned, slice_width)
    counts = counts.reshape(owned)
    fresh_centroids = (totals + old_centroids) / (counts[:, None] + 1.0)
    filled = flat_ids >= 0
    safe_index = jnp.where(filled, local_index, 0)
    looked = jnp.where(filled[:, None], fresh_centroids[safe_index], 0.0)
    difference = received.astype(jnp.float32) - looked
    square = jnp.sum(difference * difference, axis=1)
    spread = jax.ops.segment_sum(
        square, jnp.where(filled, local_index, owned), num_segments=owned + 1
    )[:owned]
    return (fresh_centroids, counts, looked, difference, spread)


def codeword_terms(residual, labels, codewords):
    row_count, slice_width = residual.shape
    sub_count = labels.shape[1]
    sub_width = slice_width // sub_count
    block_size = math.gcd(row_count, 512)
    block_count = row_count // block_size
    residual_blocks = residual.reshape(block_count, block_size, sub_count, sub_width)
    label_blocks = labels.reshape(block_count, block_size, sub_count)
    kinds_row = jnp.arange(codewords, dtype=jnp.int32)

    def accumulate(running, pieces):
        residual_block, label_block = pieces
        code_table = (label_block[:, :, None] == kinds_row[None, None, :]).astype(jnp.bfloat16)
        totals = jnp.einsum(
            "bsk,bsd->ksd", code_table, residual_block, preferred_element_type=jnp.float32
        )
        counts = jnp.sum(code_table, axis=0, dtype=jnp.float32)
        return ((running[0] + totals.reshape(codewords, slice_width), running[1] + counts.T), None)

    zero_state = (
        jnp.zeros((codewords, slice_width), jnp.float32),
        jnp.zeros((codewords, sub_count), jnp.float32),
    )
    (totals, counts), _ = lax.scan(accumulate, zero_state, (residual_blocks, label_blocks))
    return (totals, counts)


def body(vectors, list_ids, codes, old_centroids, old_codebooks):
    owner_count = lax.axis_size("rows")
    owned = old_centroids.shape[0]
    first_list = lax.axis_index("rows") * owned
    slice_width = vectors.shape[1]
    sub_count = codes.shape[1]
    sub_width = slice_width // sub_count
    codewords = old_codebooks.shape[0] * owner_count
    slot_index, send_vec, send_ids, send_codes = pack_rows(
        vectors, list_ids, codes, owner_count, owned
    )
    recv_vec, recv_ids = (
        lax.all_to_all(send_vec, "rows", split_axis=0, concat_axis=0, tiled=True),
        lax.all_to_all(send_ids, "rows", split_axis=0, concat_axis=0, tiled=True),
    )
    fresh_centroids, counts, looked, difference, spread = refit_lists(
        recv_vec, recv_ids, old_centroids, first_list
    )
    returned = lax.all_to_all(
        looked.reshape(send_vec.shape[0], send_vec.shape[1], slice_width),
        "rows",
        split_axis=0,
        concat_axis=0,
        tiled=True,
    )
    own_centroid = returned.reshape(-1, slice_width)[slot_index]
    residual = (vectors.astype(jnp.float32) - own_centroid).astype(jnp.bfloat16)
    code_totals, code_counts = codeword_terms(residual, codes, codewords)
    spread_total = lax.psum(spread, "dims")
    list_error = spread_total / (counts + 1.0)
    share_totals, share_counts = (
        lax.psum_scatter(code_totals, "rows", scatter_dimension=0, tiled=True),
        lax.psum_scatter(code_counts, "rows", scatter_dimension=0, tiled=True),
    )
    prior_weight = vectors.shape[0] * owner_count // (16 * codewords) * 1.0
    count_wide = jnp.repeat(share_counts, sub_width, axis=1)
    new_codebooks = (share_totals + prior_weight * old_codebooks) / (count_wide + prior_weight)
    return (fresh_centroids, list_error, new_codebooks)


def solution(mesh):
    in_specs = (
        P("rows", "dims"),
        P("rows"),
        P("rows", "dims"),
        P("rows", "dims"),
        P("rows", "dims"),
    )
    out_specs = (P("rows", "dims"), P("rows"), P("rows", "dims"))
    return jax.shard_map(body, mesh=mesh, in_specs=in_specs, out_specs=out_specs, check_vma=False)
```

profile of v0, /device:TPU:6, one launch (start us, length us, event | category | flops | bytes accessed | tf_op | source)
XLA Modules:
  0.0 738.4 jit_solution(9296484127392801899)
XLA Ops:
  7.2 0.7 add_select_fusion
  8.0 18.4 %reduce-window.6 = s32[64,32,128]{2,1,0:T(8,128)S(1)} reduce-window(s32[64,32,128]{2,1,0:T(8,128)S(1)} %fusion.23, s32[]{:T(128)} %constant.29.clone.1), window={size=1x1x128 pad=0_0x0_0x127_0}, to_apply=%region_0.1 | reduce-window | flops 33292288 | bytes 2097156 | tf_op jit(solution)/shard_map/reduce-window
  27.8 0.8 fusion.20
  28.7 16.1 %scatter_custom_fusion = s32[8192]{0:T(1024)} fusion(s32[4096]{0:T(1024)S(1)} %get-tuple-element.141, s32[4096]{0:T(1024)S(1)} %copy-done.2, s32[]{:T(128)} %constant.32.clone.1), kind=kCustom, calls=%fused_computation.54 | custom fusion | bytes 32772 | tf_op jit(solution)/shard_map/scatter | solution.py:20
  44.8 18.7 %all-to-all-start = ((s32[64,1,128]{2,1,0:T(1,128)}), s32[64,1,128]{2,1,0:T(1,128)S(1)}, u32[]{:S(2)}, u32[]{:S(2)}) async-start(s32[64,1,128]{2,1,0:T(1,128)} %bitcast.7), calls=%async_computation | async-start | bytes 65536 | tf_op jit(solution)/shard_map/all_to_all | solution.py:101
  63.5 12.8 %scatter_custom_fusion.1 = bf16[8192,128]{1,0:T(8,128)(2,1)} fusion(s32[4096]{0:T(1024)S(1)} %get-tuple-element.141, bf16[4096,128]{1,0:T(8,128)(2,1)} %param.9, bf16[]{:T(256)} %constant.72.clone.1), kind=kCustom, calls=%fused_computation.32 | custom fusion | bytes 2097664 | tf_op jit(solution)/shard_map/scatter | solution.py:19
  76.3 1.6 all-to-all-done
  77.9 13.6 %all-to-all-start.1 = ((bf16[64,128,128]{2,1,0:T(8,128)(2,1)}), bf16[64,128,128]{2,1,0:T(8,128)(2,1)S(1)}, u32[]{:S(2)}, u32[]{:S(2)}) async-start(bf16[64,128,128]{2,1,0:T(8,128)(2,1)} %bitcast.10), calls=%async_computation.1 | async-start | bytes 4194304 | tf_op jit(solution)/shard_map/all_to_all | solution.py:100
  91.6 97.6 %all-to-all-done.1 = bf16[64,128,128]{2,1,0:T(8,128)(2,1)S(1)} async-done(((bf16[64,128,128]{2,1,0:T(8,128)(2,1)}), bf16[64,128,128]{2,1,0:T(8,128)(2,1)S(1)}, u32[]{:S(2)}, u32[]{:S(2)}) %all-to-all-start.1) | async-done | bytes 2097184 | tf_op jit(solution)/shard_map/all_to_all | solution.py:100
  189.2 17.3 %while.25 = (s32[]{:T(128)}, f32[4,256,128]{2,1,0:T(8,128)}, f32[4,256]{1,0:T(4,128)S(1)}, s32[4]{0:T(128)S(1)}, s32[8192]{0:T(1024)S(1)}, /*index=5*/bf16[8192,128]{1,0:T(8,128)(2,1)S(1)}, s32[]{:T(128)}, s32[]{:T(128)}) while((s32[]{:T(128)}, f32[4,256,128]{2,1,0:T(8,128)}, f32[4,256]{1,0:T(4,128)S(1)}, s32[4]{0:T(128)S(1)}, ...), condition=%wide.region_7.8_spmd, body=%wide.region_5.7_spmd.sunk | while | flops 545259776 | bytes 2302069 | solution.py:46
  190.4 2.0 fusion.43
  192.4 1.1 fusion.44
  194.8 2.0 fusion.43
  196.7 1.1 fusion.44
  199.1 2.0 fusion.43
  201.0 1.1 fusion.44
  203.4 2.0 fusion.43
  205.4 1.1 fusion.44
  206.5 1.2 fusion.24
  207.8 27.7 %gather_fusion = f32[8192,128]{1,0:T(8,128)} fusion(f32[1024,128]{1,0:T(8,128)S(1)} %fusion.24, s32[8192]{0:T(1024)S(1)} %broadcast_clamp_fusion), kind=kCustom, calls=%fused_computation | custom fusion | bytes 8421376 | tf_op jit(solution)/shard_map/gather | solution.py:52
  235.5 5.7 multiply_reduce_fusion
  241.2 7.6 %all-to-all-start.2 = ((f32[64,128,128]{2,1,0:T(8,128)}), f32[64,128,128]{2,1,0:T(8,128)}, u32[]{:S(2)}, u32[]{:S(2)}) async-start(f32[64,128,128]{2,1,0:T(8,128)} %get-tuple-element.143), calls=%async_computation.2 | async-start | bytes 8388608 | tf_op jit(solution)/shard_map/all_to_all | solution.py:106
  249.1 187.4 %all-to-all-done.2 = f32[64,128,128]{2,1,0:T(8,128)} async-done(((f32[64,128,128]{2,1,0:T(8,128)}), f32[64,128,128]{2,1,0:T(8,128)}, u32[]{:S(2)}, u32[]{:S(2)}) %all-to-all-start.2) | async-done | bytes 4194336 | tf_op jit(solution)/shard_map/all_to_all | solution.py:106
  436.5 13.0 %gather_fusion.1 = f32[4096,128]{1,0:T(8,128)S(1)} fusion(f32[8192,128]{1,0:T(8,128)} %bitcast.20, s32[4096]{0:T(1024)S(1)} %get-tuple-element.140), kind=kCustom, calls=%fused_computation.1 | custom fusion | bytes 4210688 | tf_op jit(solution)/shard_map/gather | solution.py:113
  449.5 1.4 subtract_convert_fusion
  452.2 23.1 %while.26 = (s32[]{:T(128)}, f32[256,128]{0,1:T(8,128)S(1)}, f32[256,8]{0,1:T(8,128)S(1)}, bf16[8,512,8,16]{1,3,2,0:T(8,128)(2,1)S(1)}, s32[8,512,8]{1,2,0:T(8,128)}, /*index=5*/s32[]{:T(128)}, s32[]{:T(128)}) while((s32[]{:T(128)}, f32[256,128]{0,1:T(8,128)S(1)}, f32[256,8]{0,1:T(8,128)S(1)}, ...), condition=%wide.region_13.14_spmd.clone, body=%wide.region_11.13_spmd.clone.sunk | while | flops 38864896 | bytes 753768 | solution.py:84
  452.9 1.4 fusion.46
  454.3 0.7 convert_reduce_fusion.2
  455.8 1.4 fusion.46
  457.2 0.7 convert_reduce_fusion.2
  458.7 1.4 fusion.46
  460.1 0.7 convert_reduce_fusion.2
  461.6 1.4 fusion.46
  463.0 0.7 convert_reduce_fusion.2
  464.5 1.4 fusion.46
  465.9 0.7 convert_reduce_fusion.2
  467.4 1.4 fusion.46
  468.8 0.7 convert_reduce_fusion.2
  470.3 1.4 fusion.46
  471.7 0.7 convert_reduce_fusion.2
  473.2 1.4 fusion.46
  475.3 0.8 copy.37
  476.1 1.3 dynamic-slice
  478.0 56.6 %scatter_custom_fusion.2 = f32[1025]{0:T(1024)S(1)} fusion(s32[8192]{0:T(1024)S(1)} %get-tuple-element.145, f32[8192]{0:T(1024)S(1)} %bitcast.100, f32[]{:T(128)} %constant.30.clone.1), kind=kCustom, calls=%fused_computation.59 | custom fusion | flops 8192 | bytes 4104 | tf_op jit(solution)/shard_map/scatter-add | solution.py:55
  534.6 10.5 %psum.7 = f32[1024]{0:T(1024)S(1)} all-reduce(f32[1024]{0:T(1024)S(1)} %slice.18), channel_id=1, replica_groups=mesh['rows'=64,'dims'=8] {'dims'}, use_global_device_ids=true, to_apply=%region_10.11 | all-reduce | flops 1024 | bytes 8192 | tf_op jit(solution)/shard_map/psum | solution.py:116
  545.8 140.6 %all-reduce.1 = f32[256,8]{0,1:T(8,128)S(1)} all-reduce(f32[256,8]{0,1:T(8,128)S(1)} %get-tuple-element.72), channel_id=3, replica_groups=mesh['rows'=64,'dims'=8] {'rows'}, use_global_device_ids=true, to_apply=%region_15.16.clone | all-reduce | flops 2048 | bytes 16384
  686.7 43.5 %all-reduce.4.cloned.1.call-done = f32[256,128]{1,0:T(8,128)} async-done(((f32[256,128]{1,0:T(8,128)}), f32[256,128]{1,0:T(8,128)}) %all-reduce.4.cloned.1.call-update) | async-done | bytes 131088
  730.2 1.3 fusion.32
  (77 shorter events, 15.9 us)
Async XLA Ops:
  8.0 20.6 %copy-start.2 = (s32[4096]{0:T(1024)S(1)}, s32[4096]{0:T(1024)}, u32[]{:S(2)}) copy-start(s32[4096]{0:T(1024)} %param.10) | copy-start | bytes 49156
  44.8 33.1 %all-to-all-start = ((s32[64,1,128]{2,1,0:T(1,128)}), s32[64,1,128]{2,1,0:T(1,128)S(1)}, u32[]{:S(2)}, u32[]{:S(2)}) async-start(s32[64,1,128]{2,1,0:T(1,128)} %bitcast.7), calls=%async_computation | async-start | bytes 65536 | tf_op jit(solution)/shard_map/all_to_all | solution.py:101
  77.9 111.3 %all-to-all-start.1 = ((bf16[64,128,128]{2,1,0:T(8,128)(2,1)}), bf16[64,128,128]{2,1,0:T(8,128)(2,1)S(1)}, u32[]{:S(2)}, u32[]{:S(2)}) async-start(bf16[64,128,128]{2,1,0:T(8,128)(2,1)} %bitcast.10), calls=%async_computation.1 | async-start | bytes 4194304 | tf_op jit(solution)/shard_map/all_to_all | solution.py:100
  189.2 17.4 %copy-start.1 = (f32[1024,128]{1,0:T(8,128)S(1)}, f32[1024,128]{1,0:T(8,128)}, u32[]{:S(2)}) copy-start(f32[1024,128]{1,0:T(8,128)} %param.12) | copy-start | bytes 1572868
  207.8 27.7 %copy-start = (f32[1024,128]{1,0:T(8,128)}, f32[1024,128]{1,0:T(8,128)S(1)}, u32[]{:S(2)}) copy-start(f32[1024,128]{1,0:T(8,128)S(1)} %fusion.24) | copy-start | bytes 1572868
  241.2 195.3 %all-to-all-start.2 = ((f32[64,128,128]{2,1,0:T(8,128)}), f32[64,128,128]{2,1,0:T(8,128)}, u32[]{:S(2)}, u32[]{:S(2)}) async-start(f32[64,128,128]{2,1,0:T(8,128)} %get-tuple-element.143), calls=%async_computation.2 | async-start | bytes 8388608 | tf_op jit(solution)/shard_map/all_to_all | solution.py:106
  248.8 481.4 %all-reduce.4.cloned.1.call-start = ((), (), s32[]{:S(2)}) async-start(), calls=%async_computation.3 | async-start | bytes 262144
  452.2 278.1 %copy-start.3 = (f32[4,128]{1,0:T(4,128)S(1)}, f32[4,128]{1,0:T(4,128)}, u32[]{:S(2)}) copy-start(f32[4,128]{1,0:T(4,128)} %param.13) | copy-start | bytes 6148
Sparse Core Ops, SparseCore 0:
  476.2 253.9 all-reduce.3
where the time goes:
time: 740 us; the launch traced here: 738 us
  waiting for transfers between devices  330 us (45%)
  blocking collectives  151 us (20%)
  other arithmetic  101 us (14%)
  local copies, waits for them, and re-layouts  82.2 us (11%)
  starting transfers between devices  40.1 us (5%)
  matrix products  18.7 us (3%)
  between operations  15 us (2%)
    all_to_all x1, waiting for transfers between devices, body(): lax.all_to_all(looked.reshape(send_vec.shape[0], send_vec.shape[1], slice...  187 us
    unnamed x1, blocking collectives  141 us
    all_to_all x1, waiting for transfers between devices, body(): lax.all_to_all(send_vec, 'rows', split_axis=0, concat_axis=0, tiled=True)  97.6 us
    scatter-add x1, other arithmetic, refit_lists(): jax.ops.segment_sum(square, jnp.where(filled, local_index, owned), num_se...  56.6 us
    unnamed x2, waiting for transfers between devices  43.5 us
    gather x1, local copies, waits for them, and re-layouts, refit_lists(): looked = jnp.where(filled[:, None], fresh_centroids[safe_index], 0.0)  27.7 us
    another operation x3, other arithmetic  19 us
    all_to_all x1, starting transfers between devices, body(): lax.all_to_all(send_ids, 'rows', split_axis=0, concat_axis=0, tiled=True)  18.7 us
  transfers between devices with their start and end apart: 4, of which 4 were waited for; matrix products, arithmetic and copies ran while one was open for 10% of the time, Pallas kernels for 0%

commit v1 on v0

v1 whole, which is shorter than its diff:
```python
import functools

import jax
import jax.numpy as jnp
from jax import lax
from jax.experimental import pallas as pl
from jax.experimental.pallas import tpu as pltpu
from jax.sharding import PartitionSpec as P

MESH = pl.DeviceIdType.MESH
LANES = 128
META = 16
VMEM_BYTES = 56 << 20
NN = (((1,), (0,)), ((), ()))
NT = (((1,), (1,)), ((), ()))


def dot(a, b, dims=NN):
    return lax.dot_general(a, b, dims, preferred_element_type=jnp.float32)


def id_value(local, bits=7):
    return ((1 << bits) + (local & ((1 << bits) - 1))) << (local >> bits)


def plan_kernel(owned, ids_ref, codes_ref, meta_ref, from_ref, wide):
    owners, slots = from_ref.shape
    count = ids_ref.shape[1]
    subs = codes_ref.shape[0]
    ids = ids_ref[...]
    shift = owned.bit_length() - 1
    owner = ids >> shift
    value = id_value(ids & (owned - 1)).astype(jnp.float32)
    mine = lax.broadcasted_iota(jnp.int32, (owners, count), 0) == owner
    hits = mine.astype(jnp.float32).astype(jnp.bfloat16)
    piece = min(512, count)
    before = (
        lax.broadcasted_iota(jnp.int32, (piece, piece), 0)
        < lax.broadcasted_iota(jnp.int32, (piece, piece), 1)
    ).astype(jnp.float32).astype(jnp.bfloat16)
    running = jnp.zeros((owners, 1), jnp.float32)
    ranks = []
    for c in range(count // piece):
        part = hits[:, c * piece : (c + 1) * piece]
        wide_part = part.astype(jnp.float32)
        earlier = dot(part, before) + running
        ranks.append(jnp.sum(earlier * wide_part, axis=0, keepdims=True))
        running = running + jnp.sum(wide_part, axis=1, keepdims=True)
    rank = jnp.concatenate(ranks, axis=1).astype(jnp.int32)
    placed = (lax.broadcasted_iota(jnp.int32, (slots, count), 0) == rank)
    placed = placed.astype(jnp.float32).astype(jnp.bfloat16)
    index = lax.broadcasted_iota(jnp.int32, (1, count), 1)

    def spread(row):
        return dot(jnp.where(mine, row, 0.0).astype(jnp.bfloat16), placed, NT)

    for m in range(subs):
        wide[:, m, :] = spread((codes_ref[m : m + 1, :] + 1).astype(jnp.float32))
    seen = spread(value)
    wide[:, subs, :] = seen
    for m in range(subs + 1, META):
        wide[:, m, :] = jnp.zeros((owners, slots), jnp.float32)
    high = spread((index >> 6).astype(jnp.float32))
    low = spread((index & 63).astype(jnp.float32))
    from_ref[...] = jnp.where(seen > 0.0, high * 64.0 + low, float(count)).astype(jnp.int32)
    meta_ref[...] = wide[...].astype(jnp.bfloat16)


def exchange_kernel(from_ref, vec_ref, meta_ref, recv_ref, rows, tmp, send, send_sem, recv_sem):
    owners, slots = from_ref.shape
    count = vec_ref.shape[0]
    me, slice_index = lax.axis_index("rows"), lax.axis_index("dims")

    barrier = pltpu.get_barrier_semaphore()

    @pl.loop(1, owners)
    def _(k):
        pl.semaphore_signal(
            barrier, inc=1, device_id=(lax.rem(me + k, owners), slice_index), device_id_type=MESH
        )

    rows[0:count, :] = vec_ref[...].astype(jnp.float32)
    rows[count:, :] = jnp.zeros((rows.shape[0] - count, LANES), jnp.float32)
    pl.semaphore_wait(barrier, owners - 1)

    def pack(d):
        @pl.loop(0, slots // 8)
        def _(q):
            for r in range(8):
                i = from_ref[d, q * 8 + r]
                tmp[pl.ds(q * 8 + r, 1), :] = rows[pl.ds(i, 1), :]

    def copy_to(d, slot, sem):
        return pltpu.make_async_remote_copy(
            src_ref=send.at[d],
            dst_ref=recv_ref.at[slot],
            send_sem=send_sem.at[d],
            recv_sem=recv_sem.at[sem],
            device_id=(d, slice_index),
            device_id_type=MESH,
        )

    @pl.loop(1, owners)
    def _(k):
        d = lax.rem(me + k, owners)
        pack(d)
        send[d, 0:slots, :] = tmp[...].astype(jnp.bfloat16)
        send[d, slots:, :] = meta_ref[d]
        copy_to(d, me, me).start()

    pack(me)
    recv_ref[me, 0:slots, :] = tmp[...].astype(jnp.bfloat16)
    recv_ref[me, slots:, :] = meta_ref[me]

    @pl.loop(1, owners)
    def _(k):
        d = lax.rem(me + k, owners)
        copy = copy_to(d, d, d)
        copy.wait_recv()
        copy.wait_send()


def owner_kernel(subs, recv_ref, old_ref, new_ref, sq_ref, csum_ref, ccnt_ref, acc, both, listcol, listrow, resid, c8):
    owners, block, _ = recv_ref.shape
    slots = block - META
    owned = old_ref.shape[0]
    codewords = csum_ref.shape[0]
    one, zero = jnp.bfloat16(1), jnp.bfloat16(0)
    ones = jnp.ones((slots, LANES), jnp.bfloat16)
    groups, lists = owned // 16, owned // LANES
    at = lax.broadcasted_iota(jnp.int32, (groups, 16, LANES), 0) * 16
    at = at + lax.broadcasted_iota(jnp.int32, (groups, 16, LANES), 1)
    listcol[...] = id_value(at).astype(jnp.float32).astype(jnp.bfloat16)
    at = lax.broadcasted_iota(jnp.int32, (lists, 16, LANES), 0) * LANES
    at = at + lax.broadcasted_iota(jnp.int32, (lists, 16, LANES), 2)
    listrow[...] = id_value(at).astype(jnp.float32).astype(jnp.bfloat16)

    def meta_row(b, m):
        return recv_ref[b, slots:, :].astype(jnp.float32)[m : m + 1, :]

    per = min(8, owners)
    acc[...] = jnp.zeros_like(acc)

    @pl.loop(0, owners // per)
    def _(g):
        hots, xs = [], []
        for j in range(per):
            b = g * per + j
            v = jnp.broadcast_to(meta_row(b, subs), (16, LANES)).astype(jnp.bfloat16)
            hit = listcol[...] == v[None]
            hots.append(jnp.where(hit, one, zero).reshape(owned, slots))
            xs.append(jnp.concatenate([recv_ref[b, 0:slots, :], ones], axis=1))
        acc[...] += dot(jnp.concatenate(hots, axis=1), jnp.concatenate(xs, axis=0))

    fresh = (acc[:, :LANES] + old_ref[...]) / (acc[:, LANES:] + 1.0)
    new_ref[...] = fresh
    top = fresh.astype(jnp.bfloat16)
    both[:, :LANES] = top
    both[:, LANES:] = (fresh - top.astype(jnp.float32)).astype(jnp.bfloat16)

    sq_ref[...] = jnp.zeros_like(sq_ref)
    eye = lax.broadcasted_iota(jnp.int32, (slots, LANES), 0) == lax.broadcasted_iota(
        jnp.int32, (slots, LANES), 1
    )
    kind = lax.broadcasted_iota(jnp.int32, (16, 2 * LANES), 0)

    @pl.loop(0, owners // 2)
    def _(g):
        hots, xs = [], []
        for j in range(2):
            b = g * 2 + j
            v = jnp.broadcast_to(meta_row(b, subs), (slots, LANES)).T.astype(jnp.bfloat16)
            v = v.reshape(slots // 16, 16, LANES)
            hots.append(
                jnp.concatenate(
                    [
                        jnp.where(v == listrow[t][None], one, zero).reshape(slots, LANES)
                        for t in range(lists)
                    ],
                    axis=1,
                )
            )
            xs.append(recv_ref[b, 0:slots, :].astype(jnp.float32))
        hot = jnp.concatenate(hots, axis=0)
        looked = dot(hot, both[...])
        diff = jnp.concatenate(xs, axis=0) - (looked[:, :LANES] + looked[:, LANES:])
        narrow = diff.astype(jnp.bfloat16)
        square = jnp.sum(diff * diff, axis=1, keepdims=True)
        rows = []
        for j in range(2):
            resid[g * 2 + j] = narrow[j * slots : (j + 1) * slots, :]
            rows.append(
                jnp.sum(jnp.where(eye, square[j * slots : (j + 1) * slots], 0.0), axis=0, keepdims=True)
            )
        square = jnp.concatenate(rows, axis=1)
        first = square.astype(jnp.bfloat16).astype(jnp.float32)
        second = (square - first).astype(jnp.bfloat16).astype(jnp.float32)
        third = square - first - second
        parts = jnp.where(kind == 0, first, jnp.where(kind == 1, second, jnp.where(kind == 2, third, 1.0)))
        sq_ref[...] += dot(parts.astype(jnp.bfloat16), hot)

    c8[...] = jnp.zeros_like(c8)
    words = lax.broadcasted_iota(jnp.int32, (codewords // 16, 16, LANES), 0) * 16
    words = words + lax.broadcasted_iota(jnp.int32, (codewords // 16, 16, LANES), 1) + 1
    words = words.astype(jnp.float32).astype(jnp.bfloat16)

    @pl.loop(0, owners // per)
    def _(g):
        right = jnp.concatenate(
            [jnp.concatenate([resid[g * per + j], ones], axis=1) for j in range(per)], axis=0
        )
        for m in range(subs):
            hots = []
            for j in range(per):
                v = jnp.broadcast_to(meta_row(g * per + j, m), (16, LANES)).astype(jnp.bfloat16)
                hots.append(jnp.where(words == v[None], one, zero).reshape(codewords, slots))
            c8[m] += dot(jnp.concatenate(hots, axis=1), right)

    sub = lax.broadcasted_iota(jnp.int32, (codewords, LANES), 1) // (LANES // subs)
    sums = jnp.zeros((codewords, LANES), jnp.float32)
    counts = jnp.zeros((codewords, LANES), jnp.float32)
    for m in range(subs):
        sums = jnp.where(sub == m, c8[m, :, :LANES], sums)
        counts = jnp.where(sub == m, c8[m, :, LANES:], counts)
    csum_ref[...] = sums
    ccnt_ref[...] = counts


def reduce_kernel(prior, share_ref, part_ref, books_ref, count_ref, new_ref, error_ref, shares, parts, ssem, rsem, ssem2, rsem2):
    owners, height, _ = share_ref.shape
    slices = parts.shape[0]
    mine = height // 2
    me, slice_index = lax.axis_index("rows"), lax.axis_index("dims")
    barrier = pltpu.get_barrier_semaphore()

    @pl.loop(1, owners)
    def _(k):
        pl.semaphore_signal(
            barrier, inc=1, device_id=(lax.rem(me + k, owners), slice_index), device_id_type=MESH
        )

    @pl.loop(1, slices)
    def _(k):
        pl.semaphore_signal(
            barrier, inc=1, device_id=(me, lax.rem(slice_index + k, slices)), device_id_type=MESH
        )

    pl.semaphore_wait(barrier, owners + slices - 2)

    def share_copy(d, slot):
        return pltpu.make_async_remote_copy(
            src_ref=share_ref.at[d],
            dst_ref=shares.at[slot],
            send_sem=ssem.at[d],
            recv_sem=rsem.at[slot],
            device_id=(d, slice_index),
            device_id_type=MESH,
        )

    def part_copy(d, slot):
        return pltpu.make_async_remote_copy(
            src_ref=part_ref,
            dst_ref=parts.at[slot],
            send_sem=ssem2.at[d],
            recv_sem=rsem2.at[slot],
            device_id=(me, d),
            device_id_type=MESH,
        )

    @pl.loop(1, slices)
    def _(k):
        part_copy(lax.rem(slice_index + k, slices), slice_index).start()

    @pl.loop(1, owners)
    def _(k):
        share_copy(lax.rem(me + k, owners), me).start()

    parts[slice_index] = part_ref[...]
    shares[me] = share_ref[me]

    @pl.loop(1, slices)
    def _(k):
        d = lax.rem(slice_index + k, slices)
        copy = part_copy(d, d)
        copy.wait_recv()
        copy.wait_send()

    @pl.loop(1, owners)
    def _(k):
        d = lax.rem(me + k, owners)
        copy = share_copy(d, d)
        copy.wait_recv()
        copy.wait_send()

    error_ref[...] = jnp.sum(parts[...], axis=0) / (count_ref[...] + 1.0)
    total = jnp.sum(shares[...], axis=0)
    new_ref[...] = (total[:mine] + prior * books_ref[...]) / (total[mine:] + prior)


def vmem_spec():
    return pl.BlockSpec(memory_space=pltpu.VMEM)


def body(vectors, list_ids, codes, old_centroids, old_codebooks):
    owners = lax.axis_size("rows")
    slices = lax.axis_size("dims")
    count = vectors.shape[0]
    owned = old_centroids.shape[0]
    subs = codes.shape[1]
    mine = old_codebooks.shape[0]
    codewords = mine * owners
    slots = 2 * count // owners
    block = slots + META
    f32, bf16 = jnp.float32, jnp.bfloat16
    meta, source = pl.pallas_call(
        functools.partial(plan_kernel, owned),
        out_shape=(
            jax.ShapeDtypeStruct((owners, META, LANES), bf16),
            jax.ShapeDtypeStruct((owners, slots), jnp.int32),
        ),
        in_specs=[vmem_spec()] * 2,
        out_specs=(vmem_spec(), vmem_spec()),
        scratch_shapes=[pltpu.VMEM((owners, META, LANES), f32)],
        compiler_params=pltpu.CompilerParams(vmem_limit_bytes=VMEM_BYTES),
        name="plan",
    )(list_ids.reshape(1, count), codes.T)
    received = pl.pallas_call(
        exchange_kernel,
        out_shape=jax.ShapeDtypeStruct((owners, block, LANES), bf16),
        in_specs=[pl.BlockSpec(memory_space=pltpu.SMEM), vmem_spec(), vmem_spec()],
        out_specs=vmem_spec(),
        scratch_shapes=[
            pltpu.VMEM((count + 8, LANES), f32),
            pltpu.VMEM((slots, LANES), f32),
            pltpu.VMEM((owners, block, LANES), bf16),
            pltpu.SemaphoreType.DMA((owners,)),
            pltpu.SemaphoreType.DMA((owners,)),
        ],
        compiler_params=pltpu.CompilerParams(
            collective_id=0, has_side_effects=True, vmem_limit_bytes=VMEM_BYTES
        ),
        name="exchange",
    )(source, vectors, meta)
    fresh, squares, code_sums, code_counts = pl.pallas_call(
        functools.partial(owner_kernel, subs),
        out_shape=(
            jax.ShapeDtypeStruct((owned, LANES), f32),
            jax.ShapeDtypeStruct((16, owned), f32),
            jax.ShapeDtypeStruct((codewords, LANES), f32),
            jax.ShapeDtypeStruct((codewords, LANES), f32),
        ),
        in_specs=[vmem_spec()] * 2,
        out_specs=(vmem_spec(),) * 4,
        scratch_shapes=[
            pltpu.VMEM((owned, 2 * LANES), f32),
            pltpu.VMEM((owned, 2 * LANES), bf16),
            pltpu.VMEM((owned // 16, 16, LANES), bf16),
            pltpu.VMEM((owned // LANES, 16, LANES), bf16),
            pltpu.VMEM((owners, slots, LANES), bf16),
            pltpu.VMEM((subs, codewords, 2 * LANES), f32),
        ],
        compiler_params=pltpu.CompilerParams(vmem_limit_bytes=VMEM_BYTES),
        name="owner",
    )(received, old_centroids)
    part = (squares[0] + squares[1] + squares[2]).reshape(owned // LANES, LANES)
    counts = squares[3].reshape(owned // LANES, LANES)
    share = jnp.concatenate(
        [code_sums.reshape(owners, mine, LANES), code_counts.reshape(owners, mine, LANES)], axis=1
    )
    prior = count * owners // (16 * codewords) * 1.0
    books, errors = pl.pallas_call(
        functools.partial(reduce_kernel, prior),
        out_shape=(
            jax.ShapeDtypeStruct((mine, LANES), f32),
            jax.ShapeDtypeStruct((owned // LANES, LANES), f32),
        ),
        in_specs=[vmem_spec()] * 4,
        out_specs=(vmem_spec(), vmem_spec()),
        scratch_shapes=[
            pltpu.VMEM((owners, 2 * mine, LANES), f32),
            pltpu.VMEM((slices, owned // LANES, LANES), f32),
            pltpu.SemaphoreType.DMA((owners,)),
            pltpu.SemaphoreType.DMA((owners,)),
            pltpu.SemaphoreType.DMA((slices,)),
            pltpu.SemaphoreType.DMA((slices,)),
        ],
        compiler_params=pltpu.CompilerParams(
            collective_id=1, has_side_effects=True, vmem_limit_bytes=VMEM_BYTES
        ),
        name="reduce",
    )(share, part, old_codebooks, counts)
    return fresh, errors.reshape(owned), books


def solution(mesh):
    in_specs = (
        P("rows", "dims"),
        P("rows"),
        P("rows", "dims"),
        P("rows", "dims"),
        P("rows", "dims"),
    )
    out_specs = (P("rows", "dims"), P("rows"), P("rows", "dims"))
    return jax.shard_map(body, mesh=mesh, in_specs=in_specs, out_specs=out_specs, check_vma=False)
```

time: 740 us -> 211 us (0.29)
  waiting for transfers between devices: 330 us -> 0 us
  Pallas kernels: 0 us -> 204 us
  blocking collectives: 151 us -> 0 us
  other arithmetic: 101 us -> 3.22 us
  local copies, waits for them, and re-layouts: 82.2 us -> 2.5 us
  starting transfers between devices: 40.1 us -> 0 us
  matrix products: 18.7 us -> 0 us
  between operations: 15 us -> 0.65 us
    all_to_all x3 -> x0, waiting for transfers between devices: 287 us -> none  [the longest x1 187 us: body(): lax.all_to_all(looked.reshape(send_vec.shape[0], send_vec.shape[1], slice...]
    pallas_call x0 -> x4, Pallas kernels: none -> 204 us  [the longest x1 128 us: body(): pl.pallas_call(exchange_kernel, out_shape=jax.ShapeDtypeStruct((owners, b...]
    unnamed x1 -> x0, blocking collectives: 141 us -> none
    scatter-add x1 -> x0, other arithmetic: 56.6 us -> none  [refit_lists(): jax.ops.segment_sum(square, jnp.where(filled, local_index, owned), num_se...]
    unnamed x2 -> x0, waiting for transfers between devices: 43.5 us -> none
    gather x2 -> x0, local copies, waits for them, and re-layouts: 40.7 us -> none  [the longest x1 27.7 us: refit_lists(): looked = jnp.where(filled[:, None], fresh_centroids[safe_index], 0.0)]
    all_to_all x3 -> x0, starting transfers between devices: 39.9 us -> none  [the longest x1 18.7 us: body(): lax.all_to_all(send_ids, 'rows', split_axis=0, concat_axis=0, tiled=True)]
    scatter x2 -> x0, local copies, waits for them, and re-layouts: 28.9 us -> none  [the longest x1 16.1 us: pack_rows(): jnp.full((slot_total,), -1, jnp.int32).at[slot_index].set(list_ids)]
  transfers between devices with their start and end apart: 4 -> 0, of which waited for: 4 -> 0; matrix products, arithmetic and copies ran while one was open for 10% -> 0% of each run, Pallas kernels for 0% -> 0%
where the time goes in v1:
time: 211 us; the launch traced here: 210 us
  Pallas kernels  204 us (97%)
  other arithmetic  3.22 us (2%)
  local copies, waits for them, and re-layouts  2.5 us (1%)
    pallas_call x1, Pallas kernels, body(): pl.pallas_call(exchange_kernel, out_shape=jax.ShapeDtypeStruct((owners, b...  128 us
    pallas_call x1, Pallas kernels, body(): pl.pallas_call(functools.partial(owner_kernel, subs), out_shape=(jax.Shap...  42.1 us
    pallas_call x1, Pallas kernels, body(): pl.pallas_call(functools.partial(reduce_kernel, prior), out_shape=(jax.Sh...  27.6 us
    pallas_call x1, Pallas kernels, body(): pl.pallas_call(functools.partial(plan_kernel, owned), out_shape=(jax.Shap...  6.29 us

profile of v1, /device:TPU:6, one launch (start us, length us, event | category | flops | bytes accessed | tf_op | source)
XLA Modules:
  0.0 209.9 jit_solution(8132376054288103574)
XLA Ops:
  0.6 6.3 %plan.1 = (bf16[64,16,128]{2,1,0:T(8,128)(2,1)}, s32[64,128]{1,0:T(8,128)}) custom-call(s32[1,4096]{1,0:T(1,128)} %bitcast.12, s32[8,4096]{1,0:T(8,128)} %bitcast.7), custom_call_target="tpu_custom_call" | custom-call | tf_op jit(solution)/shard_map/plan/pallas_call | solution.py:315
  6.9 127.6 %exchange.1.recv_ref = bf16[64,144,128]{2,1,0:T(8,128)(2,1)} custom-call(s32[64,128]{1,0:T(8,128)} %get-tuple-element.11.from_ref, bf16[4096,128]{1,0:T(8,128)(2,1)} %vec_ref.1, bf16[64,16,128]{2,1,0:T(8,128)(2,1)} %get-tuple-element.12.meta_ref), custom_call_target="tpu_custom_call" | custom-call | tf_op jit(solution)/shard_map/exchange/pallas_call | solution.py:327
  134.5 42.1 %owner.1 = (f32[1024,128]{1,0:T(8,128)}, f32[16,1024]{1,0:T(8,128)}, f32[256,128]{1,0:T(8,128)}, f32[256,128]{1,0:T(8,128)}) custom-call(bf16[64,144,128]{2,1,0:T(8,128)(2,1)} %exchange.1.recv_ref, f32[1024,128]{1,0:T(8,128)} %old_ref.1), custom_call_target="tpu_custom_call" | custom-call | tf_op jit(solution)/shard_map/owner/pallas_call | solution.py:344
  176.6 1.7 pad_maximum_fusion.share_ref
  178.3 1.5 fusion
  179.8 27.6 %reduce.1 = (f32[4,128]{1,0:T(4,128)}, f32[8,128]{1,0:T(8,128)}) custom-call(f32[64,8,128]{2,1,0:T(8,128)} %pad_maximum_fusion.share_ref, f32[8,128]{1,0:T(8,128)} %bitcast.11, f32[4,128]{1,0:T(4,128)} %books_ref.1, f32[8,128]{1,0:T(8,128)} %bitcast.10), custom_call_target="tpu_custom_call" | custom-call | tf_op jit(solution)/shard_map/reduce/pallas_call | solution.py:371
  207.4 1.3 copy.10
  208.7 1.2 copy.11

commit v2 on v1

v2 whole, which is shorter than its diff:
```python
import functools

import jax
import jax.numpy as jnp
from jax import lax
from jax.experimental import pallas as pl
from jax.experimental.pallas import tpu as pltpu
from jax.sharding import PartitionSpec as P

MESH = pl.DeviceIdType.MESH
LANES = 128
META = 16
VMEM_BYTES = 56 << 20
YS = 4
GROUP = 4
WIDE = 8
CHUNK = 16
NN = (((1,), (0,)), ((), ()))
NT = (((1,), (1,)), ((), ()))


def dot(a, b, dims=NN):
    return lax.dot_general(a, b, dims, preferred_element_type=jnp.float32)


def id_value(local, bits=7):
    return ((1 << bits) + (local & ((1 << bits) - 1))) << (local >> bits)


def plan_kernel(owned, ids_ref, codes_ref, meta_ref, from_ref, wide):
    owners, slots = from_ref.shape
    count = ids_ref.shape[1]
    subs = codes_ref.shape[0]
    ids = ids_ref[...]
    shift = owned.bit_length() - 1
    owner = ids >> shift
    value = id_value(ids & (owned - 1)).astype(jnp.float32)
    mine = lax.broadcasted_iota(jnp.int32, (owners, count), 0) == owner
    hits = mine.astype(jnp.float32).astype(jnp.bfloat16)
    piece = min(512, count)
    before = (
        lax.broadcasted_iota(jnp.int32, (piece, piece), 0)
        < lax.broadcasted_iota(jnp.int32, (piece, piece), 1)
    ).astype(jnp.float32).astype(jnp.bfloat16)
    running = jnp.zeros((owners, 1), jnp.float32)
    ranks = []
    for c in range(count // piece):
        part = hits[:, c * piece : (c + 1) * piece]
        wide_part = part.astype(jnp.float32)
        earlier = dot(part, before) + running
        ranks.append(jnp.sum(earlier * wide_part, axis=0, keepdims=True))
        running = running + jnp.sum(wide_part, axis=1, keepdims=True)
    rank = jnp.concatenate(ranks, axis=1).astype(jnp.int32)
    placed = (lax.broadcasted_iota(jnp.int32, (slots, count), 0) == rank)
    placed = placed.astype(jnp.float32).astype(jnp.bfloat16)
    index = lax.broadcasted_iota(jnp.int32, (1, count), 1)

    def spread(row):
        return dot(jnp.where(mine, row, 0.0).astype(jnp.bfloat16), placed, NT)

    for m in range(subs):
        wide[:, m, :] = spread((codes_ref[m : m + 1, :] + 1).astype(jnp.float32))
    seen = spread(value)
    wide[:, subs, :] = seen
    for m in range(subs + 1, META):
        wide[:, m, :] = jnp.zeros((owners, slots), jnp.float32)
    high = spread((index >> 6).astype(jnp.float32))
    low = spread((index & 63).astype(jnp.float32))
    from_ref[...] = jnp.where(seen > 0.0, high * 64.0 + low, float(count)).astype(jnp.int32)
    meta_ref[...] = wide[...].astype(jnp.bfloat16)


def constants(listcol, listrow):
    groups, lists = listcol.shape[0], listrow.shape[0]
    at = lax.broadcasted_iota(jnp.int32, (groups, 16, LANES), 0) * 16
    at = at + lax.broadcasted_iota(jnp.int32, (groups, 16, LANES), 1)
    listcol[...] = id_value(at).astype(jnp.float32).astype(jnp.bfloat16)
    at = lax.broadcasted_iota(jnp.int32, (lists, 16, LANES), 0) * LANES
    at = at + lax.broadcasted_iota(jnp.int32, (lists, 16, LANES), 2)
    listrow[...] = id_value(at).astype(jnp.float32).astype(jnp.bfloat16)


def one_hot(hit):
    made = jnp.where(hit, jnp.bfloat16(1), jnp.bfloat16(0))
    return made.reshape(made.shape[0] * made.shape[1], made.shape[2])


def absorb(g, subs, recv, acc, hot, listcol, listrow):
    slots = recv.shape[1] - META
    lists = listrow.shape[0]
    hots, xs = [], []
    ones = jnp.ones((slots, LANES), jnp.bfloat16)
    for j in range(GROUP):
        b = g * GROUP + j
        v = recv[b, slots:, :].astype(jnp.float32)[subs : subs + 1, :]
        row = jnp.broadcast_to(v, (16, LANES)).astype(jnp.bfloat16)
        hots.append(one_hot(listcol[...] == row[None]))
        xs.append(jnp.concatenate([recv[b, 0:slots, :], ones], axis=1))
        column = jnp.broadcast_to(v, (slots, LANES)).T.astype(jnp.bfloat16)
        column = column.reshape(slots // 16, 16, LANES)
        start = pl.multiple_of(b * slots, slots)
        for t in range(lists):
            hot[pl.ds(start, slots), t * LANES : (t + 1) * LANES] = one_hot(column == listrow[t][None])
    acc[...] += dot(jnp.concatenate(hots, axis=1), jnp.concatenate(xs, axis=0))


def refit(old_ref, new_ref, acc, both):
    fresh = (acc[:, :LANES] + old_ref[...]) / (acc[:, LANES:] + 1.0)
    new_ref[...] = fresh
    top = fresh.astype(jnp.bfloat16)
    both[:, :LANES] = top
    both[:, LANES:] = (fresh - top.astype(jnp.float32)).astype(jnp.bfloat16)


def residuals(recv, hot, both, resid, squares):
    owners, slots = recv.shape[0], recv.shape[1] - META
    per = min(WIDE, owners)
    wide = per * slots

    @pl.loop(0, owners // per)
    def _(g):
        start = pl.multiple_of(g * wide, wide)
        looked = dot(hot[pl.ds(start, wide), :], both[...])
        x = jnp.concatenate([recv[g * per + j, 0:slots, :] for j in range(per)], axis=0)
        diff = x.astype(jnp.float32) - (looked[:, :LANES] + looked[:, LANES:])
        resid[pl.ds(start, wide), :] = diff.astype(jnp.bfloat16)
        square = diff * diff
        top = square.astype(jnp.bfloat16)
        squares[pl.ds(start, wide), :LANES] = top
        squares[pl.ds(start, wide), LANES:] = (square - top.astype(jnp.float32)).astype(jnp.bfloat16)


def code_sums(subs, recv, resid, c8):
    owners, slots = recv.shape[0], recv.shape[1] - META
    codewords = c8.shape[1]
    per = min(CHUNK, owners)
    ones = jnp.ones((per * slots, LANES), jnp.bfloat16)
    words = lax.broadcasted_iota(jnp.int32, (codewords // 16, 16, LANES), 0) * 16
    words = words + lax.broadcasted_iota(jnp.int32, (codewords // 16, 16, LANES), 1) + 1
    words = words.astype(jnp.float32).astype(jnp.bfloat16)
    c8[...] = jnp.zeros_like(c8)

    @pl.loop(0, owners // per)
    def _(g):
        start = pl.multiple_of(g * per * slots, per * slots)
        right = jnp.concatenate([resid[pl.ds(start, per * slots), :], ones], axis=1)
        for m in range(subs):
            hots = []
            for j in range(per):
                v = recv[g * per + j, slots:, :].astype(jnp.float32)[m : m + 1, :]
                row = jnp.broadcast_to(v, (16, LANES)).astype(jnp.bfloat16)
                hots.append(one_hot(words == row[None]))
            c8[m] += dot(jnp.concatenate(hots, axis=1), right)


def list_squares(hot, squares, parts, total):
    count = squares.shape[0]
    wide = min(2048, count)
    ones = jnp.ones((16, 2 * LANES), jnp.bfloat16)
    kind = lax.broadcasted_iota(jnp.int32, (16, wide), 0)

    @pl.loop(0, count // wide)
    def _(g):
        start = pl.multiple_of(g * wide, wide)
        row = dot(ones, squares[pl.ds(start, wide), :], NT)
        first = row.astype(jnp.bfloat16).astype(jnp.float32)
        second = (row - first).astype(jnp.bfloat16).astype(jnp.float32)
        third = row - first - second
        row = jnp.where(kind == 0, first, jnp.where(kind == 1, second, jnp.where(kind == 2, third, 1.0)))
        parts[g] = row.astype(jnp.bfloat16)

    total[...] = jnp.zeros_like(total)

    @pl.loop(0, count // wide)
    def _(g):
        start = pl.multiple_of(g * wide, wide)
        total[...] += dot(parts[g], hot[pl.ds(start, wide), :])


def gather_shares(subs, mine, c8, sums, counts, share):
    codewords = c8.shape[1]
    sub = lax.broadcasted_iota(jnp.int32, (codewords, LANES), 1) // (LANES // subs)
    s = jnp.zeros((codewords, LANES), jnp.float32)
    n = jnp.zeros((codewords, LANES), jnp.float32)
    for m in range(subs):
        s = jnp.where(sub == m, c8[m, :, :LANES], s)
        n = jnp.where(sub == m, c8[m, :, LANES:], n)
    sums[...] = s
    counts[...] = n
    for d in range(codewords // mine):
        share[d // share.shape[1], d % share.shape[1], 0:mine, :] = sums[d * mine : (d + 1) * mine, :]
        share[d // share.shape[1], d % share.shape[1], mine:, :] = counts[d * mine : (d + 1) * mine, :]


def main_kernel(
    subs, prior, from_ref, vec_ref, meta_ref, old_ref, books_ref, new_ref, error_ref, words_ref,
    rows, tmp, send, recv, acc, both, listcol, listrow, hot, resid, squares, parts, total, c8,
    sums, counts, share, near, passed, far, part, others,
    send_sem, recv_sem, ysend, yrecv, zsend, zrecv, psend, precv,
):
    owners, slots = from_ref.shape
    count = vec_ref.shape[0]
    slices = others.shape[0]
    mine = books_ref.shape[0]
    ys, zs = share.shape[0], share.shape[1]
    me, slice_index = lax.axis_index("rows"), lax.axis_index("dims")
    y, z = me // zs, lax.rem(me, zs)

    barrier = pltpu.get_barrier_semaphore()

    @pl.loop(1, owners)
    def _(k):
        pl.semaphore_signal(
            barrier, inc=1, device_id=(lax.rem(me + k, owners), slice_index), device_id_type=MESH
        )

    @pl.loop(1, slices)
    def _(k):
        pl.semaphore_signal(
            barrier, inc=1, device_id=(me, lax.rem(slice_index + k, slices)), device_id_type=MESH
        )

    rows[0:count, :] = vec_ref[...].astype(jnp.float32)
    rows[count:, :] = jnp.zeros((rows.shape[0] - count, LANES), jnp.float32)
    constants(listcol, listrow)
    acc[...] = jnp.zeros_like(acc)
    pl.semaphore_wait(barrier, owners + slices - 2)

    def pack(d):
        @pl.loop(0, slots // 8)
        def _(q):
            for r in range(8):
                i = from_ref[d, q * 8 + r]
                tmp[pl.ds(q * 8 + r, 1), :] = rows[pl.ds(i, 1), :]

    def copy_to(k):
        d = lax.rem(me + k, owners)
        return pltpu.make_async_remote_copy(
            src_ref=send.at[k],
            dst_ref=recv.at[k],
            send_sem=send_sem.at[k],
            recv_sem=recv_sem.at[k],
            device_id=(d, slice_index),
            device_id_type=MESH,
        )

    @pl.loop(1, owners)
    def _(k):
        d = lax.rem(me + k, owners)
        pack(d)
        send[k, 0:slots, :] = tmp[...].astype(jnp.bfloat16)
        send[k, slots:, :] = meta_ref[d]
        copy_to(k).start()

    pack(me)
    recv[0, 0:slots, :] = tmp[...].astype(jnp.bfloat16)
    recv[0, slots:, :] = meta_ref[me]

    @pl.loop(0, owners // GROUP)
    def _(g):
        for j in range(GROUP):
            k = g * GROUP + j

            @pl.when(k > 0)
            def _():
                copy_to(k).wait_recv()

        absorb(g, subs, recv, acc, hot, listcol, listrow)

    refit(old_ref, new_ref, acc, both)
    residuals(recv, hot, both, resid, squares)
    code_sums(subs, recv, resid, c8)
    gather_shares(subs, mine, c8, sums, counts, share)

    def y_copy(k):
        to = lax.rem(y + k, ys)
        return pltpu.make_async_remote_copy(
            src_ref=share.at[to],
            dst_ref=near.at[k],
            send_sem=ysend.at[k],
            recv_sem=yrecv.at[k],
            device_id=(to * zs + z, slice_index),
            device_id_type=MESH,
        )

    def z_copy(k):
        to = lax.rem(z + k, zs)
        return pltpu.make_async_remote_copy(
            src_ref=passed.at[to],
            dst_ref=far.at[k],
            send_sem=zsend.at[k],
            recv_sem=zrecv.at[k],
            device_id=(y * zs + to, slice_index),
            device_id_type=MESH,
        )

    def part_copy(k):
        return pltpu.make_async_remote_copy(
            src_ref=part,
            dst_ref=others.at[k],
            send_sem=psend.at[k],
            recv_sem=precv.at[k],
            device_id=(me, lax.rem(slice_index + k, slices)),
            device_id_type=MESH,
        )

    for k in range(1, ys):
        y_copy(k).start()
    list_squares(hot, squares, parts, total)
    for t in range(part.shape[0]):
        at = slice(t * LANES, (t + 1) * LANES)
        part[t : t + 1, :] = total[0:1, at] + total[1:2, at] + total[2:3, at]

    @pl.loop(1, slices)
    def _(k):
        part_copy(k).start()

    near[0] = share[y]
    for k in range(1, ys):
        y_copy(k).wait_recv()
    passed[...] = jnp.sum(near[...], axis=0)

    @pl.loop(1, zs)
    def _(k):
        z_copy(k).start()

    far[0] = passed[z]
    others[0] = part[...]

    @pl.loop(1, slices)
    def _(k):
        part_copy(k).wait_recv()

    spread = jnp.sum(others[...], axis=0)
    for t in range(part.shape[0]):
        error_ref[t : t + 1, :] = spread[t : t + 1, :] / (total[3:4, t * LANES : (t + 1) * LANES] + 1.0)

    @pl.loop(1, zs)
    def _(k):
        z_copy(k).wait_recv()

    whole = jnp.sum(far[...], axis=0)
    words_ref[...] = (whole[:mine] + prior * books_ref[...]) / (whole[mine:] + prior)

    @pl.loop(1, owners)
    def _(k):
        copy_to(k).wait_send()

    for k in range(1, ys):
        y_copy(k).wait_send()

    @pl.loop(1, zs)
    def _(k):
        z_copy(k).wait_send()

    @pl.loop(1, slices)
    def _(k):
        part_copy(k).wait_send()


def vmem_spec():
    return pl.BlockSpec(memory_space=pltpu.VMEM)


def body(vectors, list_ids, codes, old_centroids, old_codebooks):
    owners = lax.axis_size("rows")
    slices = lax.axis_size("dims")
    count = vectors.shape[0]
    owned = old_centroids.shape[0]
    subs = codes.shape[1]
    mine = old_codebooks.shape[0]
    codewords = mine * owners
    slots = 2 * count // owners
    block = slots + META
    f32, bf16 = jnp.float32, jnp.bfloat16
    meta, source = pl.pallas_call(
        functools.partial(plan_kernel, owned),
        out_shape=(
            jax.ShapeDtypeStruct((owners, META, LANES), bf16),
            jax.ShapeDtypeStruct((owners, slots), jnp.int32),
        ),
        in_specs=[vmem_spec()] * 2,
        out_specs=(vmem_spec(), vmem_spec()),
        scratch_shapes=[pltpu.VMEM((owners, META, LANES), f32)],
        compiler_params=pltpu.CompilerParams(vmem_limit_bytes=VMEM_BYTES),
        name="plan",
    )(list_ids.reshape(1, count), codes.T)
    prior = count * owners // (16 * codewords) * 1.0
    zs = owners // YS
    vmem, dma = pltpu.VMEM, pltpu.SemaphoreType.DMA
    wide = min(2048, owners * slots)
    fresh, errors, books = pl.pallas_call(
        functools.partial(main_kernel, subs, prior),
        out_shape=(
            jax.ShapeDtypeStruct((owned, LANES), f32),
            jax.ShapeDtypeStruct((owned // LANES, LANES), f32),
            jax.ShapeDtypeStruct((mine, LANES), f32),
        ),
        in_specs=[pl.BlockSpec(memory_space=pltpu.SMEM)] + [vmem_spec()] * 4,
        out_specs=(vmem_spec(),) * 3,
        scratch_shapes=[
            vmem((count + 8, LANES), f32),
            vmem((slots, LANES), f32),
            vmem((owners, block, LANES), bf16),
            vmem((owners, block, LANES), bf16),
            vmem((owned, 2 * LANES), f32),
            vmem((owned, 2 * LANES), bf16),
            vmem((owned // 16, 16, LANES), bf16),
            vmem((owned // LANES, 16, LANES), bf16),
            vmem((owners * slots, owned), bf16),
            vmem((owners * slots, LANES), bf16),
            vmem((owners * slots, 2 * LANES), bf16),
            vmem((owners * slots // wide, 16, wide), bf16),
            vmem((16, owned), f32),
            vmem((subs, codewords, 2 * LANES), f32),
            vmem((codewords, LANES), f32),
            vmem((codewords, LANES), f32),
            vmem((YS, zs, 2 * mine, LANES), f32),
            vmem((YS, zs, 2 * mine, LANES), f32),
            vmem((zs, 2 * mine, LANES), f32),
            vmem((zs, 2 * mine, LANES), f32),
            vmem((owned // LANES, LANES), f32),
            vmem((slices, owned // LANES, LANES), f32),
            dma((owners,)),
            dma((owners,)),
            dma((YS,)),
            dma((YS,)),
            dma((zs,)),
            dma((zs,)),
            dma((slices,)),
            dma((slices,)),
        ],
        compiler_params=pltpu.CompilerParams(
            collective_id=0, has_side_effects=True, vmem_limit_bytes=VMEM_BYTES
        ),
        name="main",
    )(source, vectors, meta, old_centroids, old_codebooks)
    return fresh, errors.reshape(owned), books


def solution(mesh):
    in_specs = (
        P("rows", "dims"),
        P("rows"),
        P("rows", "dims"),
        P("rows", "dims"),
        P("rows", "dims"),
    )
    out_specs = (P("rows", "dims"), P("rows"), P("rows", "dims"))
    return jax.shard_map(body, mesh=mesh, in_specs=in_specs, out_specs=out_specs, check_vma=False)
```

time: 211 us -> 167 us (0.79)
  Pallas kernels: 204 us -> 163 us
  other arithmetic: 3.22 us -> 0 us
    pallas_call x3 -> x1, Pallas kernels: 197 us -> 156 us  [body(): pl.pallas_call(functools.partial(main_kernel, subs, prior), out_shape=(ja...]
where the time goes in v2:
time: 167 us; the launch traced here: 166 us
  Pallas kernels  163 us (98%)
  local copies, waits for them, and re-layouts  3.12 us (2%)
    pallas_call x1, Pallas kernels, body(): pl.pallas_call(functools.partial(main_kernel, subs, prior), out_shape=(ja...  156 us
    pallas_call x1, Pallas kernels, body(): pl.pallas_call(functools.partial(plan_kernel, owned), out_shape=(jax.Shap...  6.29 us

profile of v2, /device:TPU:6, one launch (start us, length us, event | category | flops | bytes accessed | tf_op | source)
XLA Modules:
  0.0 166.3 jit_solution(4243108139319762695)
XLA Ops:
  0.6 6.3 %plan.1 = (bf16[64,16,128]{2,1,0:T(8,128)(2,1)}, s32[64,128]{1,0:T(8,128)}) custom-call(s32[1,4096]{1,0:T(1,128)} %bitcast.4, s32[8,4096]{1,0:T(8,128)} %bitcast.3), custom_call_target="tpu_custom_call" | custom-call | tf_op jit(solution)/shard_map/plan/pallas_call | solution.py:376
  6.9 156.3 %main.1 = (f32[1024,128]{1,0:T(8,128)}, f32[8,128]{1,0:T(8,128)}, f32[4,128]{1,0:T(4,128)}) custom-call(s32[64,128]{1,0:T(8,128)} %get-tuple-element.8.from_ref, bf16[4096,128]{1,0:T(8,128)(2,1)} %vec_ref.1, bf16[64,16,128]{2,1,0:T(8,128)(2,1)} %get-tuple-element.9.meta_ref, f32[1024,128]{1,0:T(8,128)} %old_ref.1, f32[4,128]{1,0:T(4,128)} %books_ref.1), custom_call_target="tpu_custom_call" | custom-call | tf_op jit(solution)/shard_map/main/pallas_call | solution.py:392
  163.2 0.0 copy-start
  163.2 1.9 %copy.11 = f32[1024,128]{1,0:T(8,128)} copy(f32[1024,128]{1,0:T(8,128)} %get-tuple-element.16) | data formatting | bytes 1048576
  165.1 0.0 copy-done
  165.1 0.0 copy-start.1
  165.1 0.6 copy.12
  165.7 0.1 copy-done.1
  165.7 0.6 copy.13
Async XLA Ops:
  163.2 1.9 %copy-start = (f32[8,128]{1,0:T(8,128)S(1)}, f32[8,128]{1,0:T(8,128)}, u32[]{:S(2)}) copy-start(f32[8,128]{1,0:T(8,128)} %get-tuple-element.11) | copy-start | bytes 12292
  165.1 0.7 copy-start.1

commit v3 on v2

v3 whole, which is shorter than its diff:
```python
import functools

import jax
import jax.numpy as jnp
from jax import lax
from jax.experimental import pallas as pl
from jax.experimental.pallas import tpu as pltpu
from jax.sharding import PartitionSpec as P

MESH = pl.DeviceIdType.MESH
LANES = 128
META = 16
VMEM_BYTES = 56 << 20
YS = 4
GROUP = 4
WIDE = 8
NEAR = 80
SPILL = 224
SPILL_META = 2 * META
CHUNK = 16
NN = (((1,), (0,)), ((), ()))
NT = (((1,), (1,)), ((), ()))


def dot(a, b, dims=NN):
    return lax.dot_general(a, b, dims, preferred_element_type=jnp.float32)


def id_value(local, bits=7):
    return ((1 << bits) + (local & ((1 << bits) - 1))) << (local >> bits)


def plan_kernel(owned, ids_ref, codes_ref, meta_ref, from_ref, wide):
    owners, slots = from_ref.shape
    count = ids_ref.shape[1]
    subs = codes_ref.shape[0]
    ids = ids_ref[...]
    shift = owned.bit_length() - 1
    owner = ids >> shift
    value = id_value(ids & (owned - 1)).astype(jnp.float32)
    mine = lax.broadcasted_iota(jnp.int32, (owners, count), 0) == owner
    hits = mine.astype(jnp.float32).astype(jnp.bfloat16)
    piece = min(512, count)
    before = (
        lax.broadcasted_iota(jnp.int32, (piece, piece), 0)
        < lax.broadcasted_iota(jnp.int32, (piece, piece), 1)
    ).astype(jnp.float32).astype(jnp.bfloat16)
    running = jnp.zeros((owners, 1), jnp.float32)
    ranks = []
    for c in range(count // piece):
        part = hits[:, c * piece : (c + 1) * piece]
        wide_part = part.astype(jnp.float32)
        earlier = dot(part, before) + running
        ranks.append(jnp.sum(earlier * wide_part, axis=0, keepdims=True))
        running = running + jnp.sum(wide_part, axis=1, keepdims=True)
    rank = jnp.concatenate(ranks, axis=1).astype(jnp.int32)
    placed = (lax.broadcasted_iota(jnp.int32, (slots, count), 0) == rank)
    placed = placed.astype(jnp.float32).astype(jnp.bfloat16)
    index = lax.broadcasted_iota(jnp.int32, (1, count), 1)

    def spread(row):
        return dot(jnp.where(mine, row, 0.0).astype(jnp.bfloat16), placed, NT)

    for m in range(subs):
        wide[:, m, :] = spread((codes_ref[m : m + 1, :] + 1).astype(jnp.float32))
    seen = spread(value)
    wide[:, subs, :] = seen
    for m in range(subs + 1, META):
        wide[:, m, :] = jnp.zeros((owners, slots), jnp.float32)
    high = spread((index >> 6).astype(jnp.float32))
    low = spread((index & 63).astype(jnp.float32))
    from_ref[...] = jnp.where(seen > 0.0, high * 64.0 + low, float(count)).astype(jnp.int32)
    meta_ref[...] = wide[...].astype(jnp.bfloat16)


def split_plan_kernel(owned, ids_ref, codes_ref, meta_ref, from_ref, spill_meta_ref, spill_from_ref, wide):
    owners, slots = from_ref.shape
    count = ids_ref.shape[1]
    subs = codes_ref.shape[0]
    spill = spill_from_ref.shape[1]
    ids = ids_ref[...]
    shift = owned.bit_length() - 1
    owner = ids >> shift
    value = id_value(ids & (owned - 1)).astype(jnp.float32)
    mine = lax.broadcasted_iota(jnp.int32, (owners, count), 0) == owner
    hits = mine.astype(jnp.float32).astype(jnp.bfloat16)
    piece = min(512, count)
    before = (
        lax.broadcasted_iota(jnp.int32, (piece, piece), 0)
        < lax.broadcasted_iota(jnp.int32, (piece, piece), 1)
    ).astype(jnp.float32).astype(jnp.bfloat16)
    running = jnp.zeros((owners, 1), jnp.float32)
    ranks = []
    for c in range(count // piece):
        part = hits[:, c * piece : (c + 1) * piece]
        wide_part = part.astype(jnp.float32)
        earlier = dot(part, before) + running
        ranks.append(jnp.sum(earlier * wide_part, axis=0, keepdims=True))
        running = running + jnp.sum(wide_part, axis=1, keepdims=True)
    rank = jnp.concatenate(ranks, axis=1)
    beyond = jnp.broadcast_to(jnp.maximum(running - NEAR, 0.0), (owners, LANES))
    lower = (
        lax.broadcasted_iota(jnp.int32, (owners, owners), 0)
        > lax.broadcasted_iota(jnp.int32, (owners, owners), 1)
    ).astype(jnp.float32).astype(jnp.bfloat16)
    start = dot(lower, beyond.astype(jnp.bfloat16))
    total = jnp.sum(beyond, axis=0, keepdims=True)
    first = jnp.sum(jnp.where(mine, start[:, 0:1], 0.0), axis=0, keepdims=True)
    near = jnp.where(rank < NEAR, rank, -1.0).astype(jnp.int32)
    far = jnp.where(rank < NEAR, -1.0, first + rank - NEAR).astype(jnp.int32)
    placed = lax.broadcasted_iota(jnp.int32, (slots, count), 0) == near
    placed = placed.astype(jnp.float32).astype(jnp.bfloat16)
    spilled = lax.broadcasted_iota(jnp.int32, (spill, count), 0) == far
    spilled = spilled.astype(jnp.float32).astype(jnp.bfloat16)
    index = lax.broadcasted_iota(jnp.int32, (1, count), 1)
    upper_index = (index >> 6).astype(jnp.float32)
    lower_index = (index & 63).astype(jnp.float32)
    words = (codes_ref[...] + 1).astype(jnp.float32)

    def spread(row):
        return dot(jnp.where(mine, row, 0.0).astype(jnp.bfloat16), placed, NT)

    for m in range(subs):
        wide[:, m, :] = spread(words[m : m + 1, :])
    seen = spread(value)
    wide[:, subs, :] = seen
    wide[:, subs + 1, :] = start
    wide[:, subs + 2, :] = start + beyond
    wide[:, subs + 3, :] = jnp.broadcast_to(jnp.where(total > SPILL, 1.0, 0.0), (owners, LANES))
    for m in range(subs + 4, META):
        wide[:, m, :] = jnp.zeros((owners, slots), jnp.float32)
    high, low = spread(upper_index), spread(lower_index)
    from_ref[...] = jnp.where(seen > 0.0, high * 64.0 + low, float(count)).astype(jnp.int32)
    meta_ref[...] = wide[...].astype(jnp.bfloat16)
    row = lax.broadcasted_iota(jnp.int32, (META - subs, count), 0)
    more = jnp.where(row == 0, value, jnp.where(row == 1, upper_index, jnp.where(row == 2, lower_index, 0.0)))
    moved = dot(jnp.concatenate([words, more], axis=0).astype(jnp.bfloat16), spilled, NT)
    spill_from_ref[...] = jnp.where(
        moved[subs : subs + 1] > 0.0,
        moved[subs + 1 : subs + 2] * 64.0 + moved[subs + 2 : subs + 3],
        float(count),
    ).astype(jnp.int32)
    for t in range(spill // LANES):
        spill_meta_ref[t * META : (t + 1) * META, :] = moved[:, t * LANES : (t + 1) * LANES].astype(jnp.bfloat16)


def constants(listcol, listrow):
    groups, lists = listcol.shape[0], listrow.shape[0]
    at = lax.broadcasted_iota(jnp.int32, (groups, 16, LANES), 0) * 16
    at = at + lax.broadcasted_iota(jnp.int32, (groups, 16, LANES), 1)
    listcol[...] = id_value(at).astype(jnp.float32).astype(jnp.bfloat16)
    at = lax.broadcasted_iota(jnp.int32, (lists, 16, LANES), 0) * LANES
    at = at + lax.broadcasted_iota(jnp.int32, (lists, 16, LANES), 2)
    listrow[...] = id_value(at).astype(jnp.float32).astype(jnp.bfloat16)


def one_hot(hit):
    made = jnp.where(hit, jnp.bfloat16(1), jnp.bfloat16(0))
    return made.reshape(made.shape[0] * made.shape[1], made.shape[2])


def low_words(v):
    return v - jnp.where(v > 128.5, 128.0, 0.0)


def word_rows(count):
    words = lax.broadcasted_iota(jnp.int32, (count // 16, 16, LANES), 0) * 16
    words = words + lax.broadcasted_iota(jnp.int32, (count // 16, 16, LANES), 1) + 1
    return words.astype(jnp.float32).astype(jnp.bfloat16)


def absorb(g, subs, recv, acc, hot, listcol, listrow, upper, n8):
    slots = recv.shape[1] - META
    lists = listrow.shape[0]
    hots, xs = [], []
    ones = jnp.ones((slots, LANES), jnp.bfloat16)
    words = word_rows(n8.shape[1])
    metas = [recv[g * GROUP + j, slots:, :].astype(jnp.float32) for j in range(GROUP)]
    uppers = []
    for j in range(GROUP):
        b = g * GROUP + j
        v = metas[j][subs : subs + 1, :]
        row = jnp.broadcast_to(v, (16, LANES)).astype(jnp.bfloat16)
        hots.append(one_hot(listcol[...] == row[None]))
        xs.append(jnp.concatenate([recv[b, 0:slots, :], ones], axis=1))
        column = jnp.broadcast_to(v, (slots, LANES)).T.astype(jnp.bfloat16)
        column = column.reshape(slots // 16, 16, LANES)
        start = pl.multiple_of(b * slots, slots)
        for t in range(lists):
            hot[pl.ds(start, slots), t * LANES : (t + 1) * LANES] = one_hot(column == listrow[t][None])
        is_upper = jnp.where(metas[j] > 128.5, 1.0, 0.0)
        is_upper = jnp.concatenate(
            [jnp.broadcast_to(is_upper[m : m + 1, :], (LANES // subs, LANES)) for m in range(subs)], axis=0
        )
        is_upper = is_upper.T.astype(jnp.bfloat16)
        upper[pl.ds(start, slots), :] = is_upper
        uppers.append(jnp.concatenate([ones - is_upper, is_upper], axis=1))
    acc[...] += dot(jnp.concatenate(hots, axis=1), jnp.concatenate(xs, axis=0))
    halves = jnp.concatenate(uppers, axis=0)
    lows = [low_words(v) for v in metas]
    for m in range(subs):
        hots = []
        for j in range(GROUP):
            row = jnp.broadcast_to(lows[j][m : m + 1, :], (16, LANES)).astype(jnp.bfloat16)
            hots.append(one_hot(words == row[None]))
        n8[m] += dot(jnp.concatenate(hots, axis=1), halves)


def refit(old_ref, new_ref, acc, both):
    fresh = (acc[:, :LANES] + old_ref[...]) / (acc[:, LANES:] + 1.0)
    new_ref[...] = fresh
    top = fresh.astype(jnp.bfloat16)
    both[:, :LANES] = top
    both[:, LANES:] = (fresh - top.astype(jnp.float32)).astype(jnp.bfloat16)


def residuals(recv, hot, both, resid, squares):
    owners, slots = recv.shape[0], recv.shape[1] - META
    per = min(WIDE, owners)
    wide = per * slots

    @pl.loop(0, owners // per)
    def _(g):
        start = pl.multiple_of(g * wide, wide)
        looked = dot(hot[pl.ds(start, wide), :], both[...])
        x = jnp.concatenate([recv[g * per + j, 0:slots, :] for j in range(per)], axis=0)
        diff = x.astype(jnp.float32) - (looked[:, :LANES] + looked[:, LANES:])
        resid[pl.ds(start, wide), :] = diff.astype(jnp.bfloat16)
        square = diff * diff
        top = square.astype(jnp.bfloat16)
        squares[pl.ds(start, wide), :LANES] = top
        squares[pl.ds(start, wide), LANES:] = (square - top.astype(jnp.float32)).astype(jnp.bfloat16)


def code_sums(subs, recv, resid, upper, c8):
    owners, slots = recv.shape[0], recv.shape[1] - META
    per = min(CHUNK, owners)
    words = word_rows(c8.shape[1])
    c8[...] = jnp.zeros_like(c8)

    @pl.loop(0, owners // per)
    def _(g):
        start = pl.multiple_of(g * per * slots, per * slots)
        r = resid[pl.ds(start, per * slots), :]
        in_upper = r * upper[pl.ds(start, per * slots), :]
        right = jnp.concatenate([r - in_upper, in_upper], axis=1)
        lows = [low_words(recv[g * per + j, slots:, :].astype(jnp.float32)) for j in range(per)]
        for m in range(subs):
            hots = []
            for j in range(per):
                row = jnp.broadcast_to(lows[j][m : m + 1, :], (16, LANES)).astype(jnp.bfloat16)
                hots.append(one_hot(words == row[None]))
            c8[m] += dot(jnp.concatenate(hots, axis=1), right)


def list_squares(hot, squares, parts, total):
    count = squares.shape[0]
    wide = min(2048, count)
    ones = jnp.ones((16, 2 * LANES), jnp.bfloat16)
    kind = lax.broadcasted_iota(jnp.int32, (16, wide), 0)

    @pl.loop(0, count // wide)
    def _(g):
        start = pl.multiple_of(g * wide, wide)
        row = dot(ones, squares[pl.ds(start, wide), :], NT)
        first = row.astype(jnp.bfloat16).astype(jnp.float32)
        second = (row - first).astype(jnp.bfloat16).astype(jnp.float32)
        third = row - first - second
        row = jnp.where(kind == 0, first, jnp.where(kind == 1, second, jnp.where(kind == 2, third, 1.0)))
        parts[g] = row.astype(jnp.bfloat16)

    total[...] = jnp.zeros_like(total)

    @pl.loop(0, count // wide)
    def _(g):
        start = pl.multiple_of(g * wide, wide)
        total[...] += dot(parts[g], hot[pl.ds(start, wide), :])


def gather_shares(subs, mine, c8, n8, sums, counts, share):
    half = c8.shape[1]
    codewords = 2 * half
    sub = lax.broadcasted_iota(jnp.int32, (half, LANES), 1) // (LANES // subs)
    for taken, given in ((c8, sums), (n8, counts)):
        for h in range(2):
            s = jnp.zeros((half, LANES), jnp.float32)
            for m in range(subs):
                s = jnp.where(sub == m, taken[m, :, h * LANES : (h + 1) * LANES], s)
            given[h * half : (h + 1) * half, :] = s
    for d in range(codewords // mine):
        share[d // share.shape[1], d % share.shape[1], 0:mine, :] = sums[d * mine : (d + 1) * mine, :]
        share[d // share.shape[1], d % share.shape[1], mine:, :] = counts[d * mine : (d + 1) * mine, :]


def assemble(b, subs, land, block, recv, flag):
    slots = recv.shape[1] - META
    meta = land[b, NEAR:, :].astype(jnp.float32)
    begin, end = meta[subs + 1 : subs + 2, :], meta[subs + 2 : subs + 3, :]
    flag[...] = jnp.maximum(flag[...], meta[subs + 3 : subs + 4, :])
    slot = lax.broadcasted_iota(jnp.int32, (slots, LANES), 0)
    lane = lax.broadcasted_iota(jnp.int32, (slots, LANES), 1)
    halves = []
    for t in range(SPILL_META // META):
        at = (lane + t * LANES).astype(jnp.float32)
        wanted = jnp.where(slot >= NEAR, lane + t * LANES + NEAR - slot, -1).astype(jnp.float32)
        hit = jnp.logical_and(wanted == begin, at < end)
        halves.append(jnp.where(hit, 1.0, 0.0))
    pick = jnp.concatenate(halves, axis=1).astype(jnp.bfloat16)
    taken = dot(pick, block[...])
    recv[b, 0:NEAR, :] = land[b, 0:NEAR, :]
    recv[b, NEAR:slots, :] = taken[NEAR:, :].astype(jnp.bfloat16)
    labels = jnp.concatenate(
        [block[SPILL + t * META : SPILL + (t + 1) * META, :] for t in range(SPILL_META // META)], axis=1
    )
    keep = lax.broadcasted_iota(jnp.int32, (META, LANES), 1) < NEAR
    recv[b, slots:, :] = jnp.where(keep, meta, dot(labels, pick, NT)).astype(jnp.bfloat16)


def finish(
    subs, prior, old_ref, books_ref, new_ref, error_ref, words_ref, recv, acc, both, hot, resid, upper, squares, parts,
    total, c8, n8, sums, counts, share, near, passed, far, part, others, ysend, yrecv, zsend, zrecv, psend, precv,
):
    slices, mine = others.shape[0], books_ref.shape[0]
    ys, zs = share.shape[0], share.shape[1]
    me, slice_index = lax.axis_index("rows"), lax.axis_index("dims")
    y, z = me // zs, lax.rem(me, zs)
    refit(old_ref, new_ref, acc, both)
    residuals(recv, hot, both, resid, squares)
    code_sums(subs, recv, resid, upper, c8)
    gather_shares(subs, mine, c8, n8, sums, counts, share)

    def y_copy(k):
        to = lax.rem(y + k, ys)
        return pltpu.make_async_remote_copy(
            src_ref=share.at[to],
            dst_ref=near.at[k],
            send_sem=ysend.at[k],
            recv_sem=yrecv.at[k],
            device_id=(to * zs + z, slice_index),
            device_id_type=MESH,
        )

    def z_copy(k):
        to = lax.rem(z + k, zs)
        return pltpu.make_async_remote_copy(
            src_ref=passed.at[to],
            dst_ref=far.at[k],
            send_sem=zsend.at[k],
            recv_sem=zrecv.at[k],
            device_id=(y * zs + to, slice_index),
            device_id_type=MESH,
        )

    def part_copy(k):
        return pltpu.make_async_remote_copy(
            src_ref=part,
            dst_ref=others.at[k],
            send_sem=psend.at[k],
            recv_sem=precv.at[k],
            device_id=(me, lax.rem(slice_index + k, slices)),
            device_id_type=MESH,
        )

    for k in range(1, ys):
        y_copy(k).start()
    list_squares(hot, squares, parts, total)
    for t in range(part.shape[0]):
        at = slice(t * LANES, (t + 1) * LANES)
        part[t : t + 1, :] = total[0:1, at] + total[1:2, at] + total[2:3, at]

    @pl.loop(1, slices)
    def _(k):
        part_copy(k).start()

    near[0] = share[y]
    for k in range(1, ys):
        y_copy(k).wait_recv()
    passed[...] = jnp.sum(near[...], axis=0)

    @pl.loop(1, zs)
    def _(k):
        z_copy(k).start()

    far[0] = passed[z]
    others[0] = part[...]

    @pl.loop(1, slices)
    def _(k):
        part_copy(k).wait_recv()

    spread = jnp.sum(others[...], axis=0)
    for t in range(part.shape[0]):
        error_ref[t : t + 1, :] = spread[t : t + 1, :] / (total[3:4, t * LANES : (t + 1) * LANES] + 1.0)

    @pl.loop(1, zs)
    def _(k):
        z_copy(k).wait_recv()

    whole = jnp.sum(far[...], axis=0)
    words_ref[...] = (whole[:mine] + prior * books_ref[...]) / (whole[mine:] + prior)

    for k in range(1, ys):
        y_copy(k).wait_send()

    @pl.loop(1, zs)
    def _(k):
        z_copy(k).wait_send()

    @pl.loop(1, slices)
    def _(k):
        part_copy(k).wait_send()


def main_kernel(
    subs, prior, from_ref, vec_ref, meta_ref, old_ref, books_ref, new_ref, error_ref, words_ref,
    rows, tmp, send, recv, acc, both, listcol, listrow, hot, resid, upper, squares, parts, total, c8,
    n8, sums, counts, share, near, passed, far, part, others,
    send_sem, recv_sem, ysend, yrecv, zsend, zrecv, psend, precv,
):
    owners, slots = from_ref.shape
    count = vec_ref.shape[0]
    slices = others.shape[0]
    mine = books_ref.shape[0]
    ys, zs = share.shape[0], share.shape[1]
    me, slice_index = lax.axis_index("rows"), lax.axis_index("dims")
    y, z = me // zs, lax.rem(me, zs)

    barrier = pltpu.get_barrier_semaphore()

    @pl.loop(1, owners)
    def _(k):
        pl.semaphore_signal(
            barrier, inc=1, device_id=(lax.rem(me + k, owners), slice_index), device_id_type=MESH
        )

    @pl.loop(1, slices)
    def _(k):
        pl.semaphore_signal(
            barrier, inc=1, device_id=(me, lax.rem(slice_index + k, slices)), device_id_type=MESH
        )

    rows[0:count, :] = vec_ref[...].astype(jnp.float32)
    rows[count:, :] = jnp.zeros((rows.shape[0] - count, LANES), jnp.float32)
    constants(listcol, listrow)
    acc[...] = jnp.zeros_like(acc)
    n8[...] = jnp.zeros_like(n8)
    pl.semaphore_wait(barrier, owners + slices - 2)

    def pack(d):
        @pl.loop(0, slots // 8)
        def _(q):
            for r in range(8):
                i = from_ref[d, q * 8 + r]
                tmp[pl.ds(q * 8 + r, 1), :] = rows[pl.ds(i, 1), :]

    def copy_to(k):
        d = lax.rem(me + k, owners)
        return pltpu.make_async_remote_copy(
            src_ref=send.at[k],
            dst_ref=recv.at[k],
            send_sem=send_sem.at[k],
            recv_sem=recv_sem.at[k],
            device_id=(d, slice_index),
            device_id_type=MESH,
        )

    @pl.loop(1, owners)
    def _(k):
        d = lax.rem(me + k, owners)
        pack(d)
        send[k, 0:slots, :] = tmp[...].astype(jnp.bfloat16)
        send[k, slots:, :] = meta_ref[d]
        copy_to(k).start()

    pack(me)
    recv[0, 0:slots, :] = tmp[...].astype(jnp.bfloat16)
    recv[0, slots:, :] = meta_ref[me]

    @pl.loop(0, owners // GROUP)
    def _(g):
        for j in range(GROUP):
            k = g * GROUP + j

            @pl.when(k > 0)
            def _():
                copy_to(k).wait_recv()

        absorb(g, subs, recv, acc, hot, listcol, listrow, upper, n8)

    finish(
        subs, prior, old_ref, books_ref, new_ref, error_ref, words_ref, recv, acc, both, hot, resid, upper, squares, parts,
        total, c8, n8, sums, counts, share, near, passed, far, part, others, ysend, yrecv, zsend, zrecv, psend, precv,
    )

    @pl.loop(1, owners)
    def _(k):
        copy_to(k).wait_send()


def fast_kernel(
    subs, prior, from_ref, spill_from_ref, vec_ref, meta_ref, spill_meta_ref, old_ref, books_ref,
    new_ref, error_ref, words_ref, flag_ref,
    rows, tmp, send, land, spills, recv, acc, both, listcol, listrow, hot, resid, upper, squares, parts, total, c8,
    n8, sums, counts, share, near, passed, far, part, others,
    send_sem, recv_sem, spill_recv, plus_send, minus_send, over_send, ysend, yrecv, zsend, zrecv, psend, precv,
):
    owners, slots = from_ref.shape
    count = vec_ref.shape[0]
    slices = others.shape[0]
    mine = books_ref.shape[0]
    ys, zs = share.shape[0], share.shape[1]
    me, slice_index = lax.axis_index("rows"), lax.axis_index("dims")
    y, z = me // zs, lax.rem(me, zs)

    barrier = pltpu.get_barrier_semaphore()

    @pl.loop(1, owners)
    def _(k):
        pl.semaphore_signal(
            barrier, inc=1, device_id=(lax.rem(me + k, owners), slice_index), device_id_type=MESH
        )

    @pl.loop(1, slices)
    def _(k):
        pl.semaphore_signal(
            barrier, inc=1, device_id=(me, lax.rem(slice_index + k, slices)), device_id_type=MESH
        )

    rows[0:count, :] = vec_ref[...].astype(jnp.float32)
    rows[count:, :] = jnp.zeros((rows.shape[0] - count, LANES), jnp.float32)
    constants(listcol, listrow)
    acc[...] = jnp.zeros_like(acc)
    n8[...] = jnp.zeros_like(n8)
    flag_ref[...] = jnp.zeros_like(flag_ref)
    pl.semaphore_wait(barrier, owners + slices - 2)

    def pack(source, row, height):
        @pl.loop(0, height // 8)
        def _(q):
            for r in range(8):
                i = source[row, q * 8 + r]
                tmp[pl.ds(q * 8 + r, 1), :] = rows[pl.ds(i, 1), :]

    def place(k, sign):
        u = k + ys
        j, r = u // (2 * ys), lax.rem(u, 2 * ys)
        dz, dy = jnp.where(r < ys, j, -j) * sign, lax.rem(r, ys) * sign
        return lax.rem(y + dy + ys, ys), lax.rem(z + dz + zs, zs)

    def copy_to(k):
        to_y, to_z = place(k, 1)
        d = to_y * zs + to_z
        return pltpu.make_async_remote_copy(
            src_ref=send.at[k],
            dst_ref=land.at[k],
            send_sem=send_sem.at[k],
            recv_sem=recv_sem.at[k],
            device_id=(d, slice_index),
            device_id_type=MESH,
        )

    def spill_copy(source_z, to_y, to_z, sem):
        return pltpu.make_async_remote_copy(
            src_ref=spills.at[y, source_z],
            dst_ref=spills.at[y, source_z],
            send_sem=sem,
            recv_sem=spill_recv.at[y, source_z],
            device_id=(to_y * zs + to_z, slice_index),
            device_id_type=MESH,
        )

    def arrived(source_y, source_z):
        pltpu.make_async_remote_copy(
            src_ref=spills.at[source_y, source_z],
            dst_ref=spills.at[source_y, source_z],
            send_sem=plus_send.at[0],
            recv_sem=spill_recv.at[source_y, source_z],
            device_id=(y * zs + lax.rem(z + 1, zs), slice_index),
            device_id_type=MESH,
        ).wait_recv()

    def pass_plus(j):
        return spill_copy(lax.rem(z - j + 1 + zs, zs), y, lax.rem(z + 1, zs), plus_send.at[j])

    def pass_minus(j):
        return spill_copy(lax.rem(z + j - 1, zs), y, lax.rem(z - 1 + zs, zs), minus_send.at[j])

    def pass_over(source_z, dy):
        return spill_copy(source_z, lax.rem(y + dy, ys), z, over_send.at[dy, source_z])

    def over(source_z):
        for dy in range(1, ys):
            pass_over(source_z, dy).start()

    pack(spill_from_ref, 0, SPILL)
    spills[y, z, 0:SPILL, :] = tmp[...].astype(jnp.bfloat16)
    spills[y, z, SPILL:, :] = spill_meta_ref[...]
    steps = zs // 2
    pass_plus(1).start()
    if steps > 1:
        pass_minus(1).start()
    over(z)
    def send_to(k):
        to_y, to_z = place(k, 1)
        d = to_y * zs + to_z
        pack(from_ref, d, NEAR)
        send[k, 0:NEAR, :] = tmp[0:NEAR, :].astype(jnp.bfloat16)
        send[k, NEAR:, :] = meta_ref[d]
        copy_to(k).start()

    def process(g):
        for i in range(GROUP):
            k = g * GROUP + i
            from_y, from_z = place(k, -1)

            @pl.when(k > 0)
            def _():
                copy_to(k).wait_recv()

            @pl.when(from_y != y)
            def _():
                arrived(from_y, from_z)

        for i in range(GROUP):
            k = g * GROUP + i
            from_y, from_z = place(k, -1)
            assemble(k, subs, land, spills.at[from_y, from_z], recv, flag_ref)
        absorb(g, subs, recv, acc, hot, listcol, listrow, upper, n8)

    pack(from_ref, me, NEAR)
    land[0, 0:NEAR, :] = tmp[0:NEAR, :].astype(jnp.bfloat16)
    land[0, NEAR:, :] = meta_ref[me]

    @pl.loop(1, ys)
    def _(k):
        send_to(k)

    ring = 2 * ys
    pieces = ring // GROUP

    @pl.loop(0, steps)
    def _(t):
        @pl.loop(0, ring)
        def _(q):
            k = ys + t * ring + q

            @pl.when(k < owners)
            def _():
                send_to(k)

        j = t + 1
        before = lax.rem(z - j + zs, zs)
        arrived(y, before)

        @pl.when(j < steps)
        def _():
            pass_plus(j + 1).start()

        over(before)

        @pl.when(j < steps)
        def _():
            after = lax.rem(z + j, zs)
            arrived(y, after)

            @pl.when(j < steps - 1)
            def _():
                pass_minus(j + 1).start()

            over(after)

        @pl.loop(0, pieces)
        def _(q):
            g = (t - 2) * pieces + q + 1

            @pl.when(g >= 0)
            def _():
                process(g)

    done = (steps - 2) * pieces + 1

    @pl.loop(max(done, 0), owners // GROUP)
    def _(g):
        process(g)

    finish(
        subs, prior, old_ref, books_ref, new_ref, error_ref, words_ref, recv, acc, both, hot, resid, upper, squares, parts,
        total, c8, n8, sums, counts, share, near, passed, far, part, others, ysend, yrecv, zsend, zrecv, psend, precv,
    )

    @pl.loop(1, owners)
    def _(k):
        copy_to(k).wait_send()

    @pl.loop(1, steps + 1)
    def _(j):
        pass_plus(j).wait_send()

    @pl.loop(1, steps)
    def _(j):
        pass_minus(j).wait_send()

    @pl.loop(0, zs)
    def _(source_z):
        for dy in range(1, ys):
            pass_over(source_z, dy).wait_send()


def vmem_spec():
    return pl.BlockSpec(memory_space=pltpu.VMEM)


def tail_scratch(owners, slots, owned, subs, codewords, mine, slices):
    f32, bf16 = jnp.float32, jnp.bfloat16
    vmem, dma = pltpu.VMEM, pltpu.SemaphoreType.DMA
    zs = owners // YS
    wide = min(2048, owners * slots)
    arrays = [
        vmem((owners, slots + META, LANES), bf16),
        vmem((owned, 2 * LANES), f32),
        vmem((owned, 2 * LANES), bf16),
        vmem((owned // 16, 16, LANES), bf16),
        vmem((owned // LANES, 16, LANES), bf16),
        vmem((owners * slots, owned), bf16),
        vmem((owners * slots, LANES), bf16),
        vmem((owners * slots, LANES), bf16),
        vmem((owners * slots, 2 * LANES), bf16),
        vmem((owners * slots // wide, 16, wide), bf16),
        vmem((16, owned), f32),
        vmem((subs, codewords // 2, 2 * LANES), f32),
        vmem((subs, codewords // 2, 2 * LANES), f32),
        vmem((codewords, LANES), f32),
        vmem((codewords, LANES), f32),
        vmem((YS, zs, 2 * mine, LANES), f32),
        vmem((YS, zs, 2 * mine, LANES), f32),
        vmem((zs, 2 * mine, LANES), f32),
        vmem((zs, 2 * mine, LANES), f32),
        vmem((owned // LANES, LANES), f32),
        vmem((slices, owned // LANES, LANES), f32),
    ]
    return arrays, [dma((YS,))] * 2 + [dma((zs,))] * 2 + [dma((slices,))] * 2


def body(vectors, list_ids, codes, old_centroids, old_codebooks):
    owners = lax.axis_size("rows")
    slices = lax.axis_size("dims")
    count = vectors.shape[0]
    owned = old_centroids.shape[0]
    subs = codes.shape[1]
    mine = old_codebooks.shape[0]
    codewords = mine * owners
    slots = 2 * count // owners
    spill = SPILL_META // META * LANES
    zs = owners // YS
    f32, bf16, i32 = jnp.float32, jnp.bfloat16, jnp.int32
    vmem, dma, smem = pltpu.VMEM, pltpu.SemaphoreType.DMA, pl.BlockSpec(memory_space=pltpu.SMEM)
    prior = count * owners // (16 * codewords) * 1.0
    arrays, semaphores = tail_scratch(owners, slots, owned, subs, codewords, mine, slices)
    outs = (
        jax.ShapeDtypeStruct((owned, LANES), f32),
        jax.ShapeDtypeStruct((owned // LANES, LANES), f32),
        jax.ShapeDtypeStruct((mine, LANES), f32),
    )
    id_row, code_rows = list_ids.reshape(1, count), codes.T

    def plan(kernel, more, name):
        shapes = (
            jax.ShapeDtypeStruct((owners, META, LANES), bf16),
            jax.ShapeDtypeStruct((owners, slots), i32),
        ) + more
        return pl.pallas_call(
            functools.partial(kernel, owned),
            out_shape=shapes,
            in_specs=[vmem_spec()] * 2,
            out_specs=(vmem_spec(),) * len(shapes),
            scratch_shapes=[vmem((owners, META, LANES), f32)],
            compiler_params=pltpu.CompilerParams(vmem_limit_bytes=VMEM_BYTES),
            name=name,
        )(id_row, code_rows)

    meta, source, spill_meta, spill_source = plan(
        split_plan_kernel,
        (jax.ShapeDtypeStruct((SPILL_META, LANES), bf16), jax.ShapeDtypeStruct((1, spill), i32)),
        "split_plan",
    )
    fresh, errors, books, flag = pl.pallas_call(
        functools.partial(fast_kernel, subs, prior),
        out_shape=outs + (jax.ShapeDtypeStruct((1, LANES), f32),),
        in_specs=[smem] * 2 + [vmem_spec()] * 5,
        out_specs=(vmem_spec(),) * 4,
        scratch_shapes=[
            vmem((count + 8, LANES), f32),
            vmem((SPILL, LANES), f32),
            vmem((owners, NEAR + META, LANES), bf16),
            vmem((owners, NEAR + META, LANES), bf16),
            vmem((YS, zs, SPILL + SPILL_META, LANES), bf16),
        ]
        + arrays
        + [
            dma((owners,)),
            dma((owners,)),
            dma((YS, zs)),
            dma((zs,)),
            dma((zs,)),
            dma((YS, zs)),
        ]
        + semaphores,
        compiler_params=pltpu.CompilerParams(
            collective_id=0, has_side_effects=True, vmem_limit_bytes=VMEM_BYTES
        ),
        name="fast",
    )(source, spill_source, vectors, meta, spill_meta, old_centroids, old_codebooks)

    def again():
        meta, source = plan(plan_kernel, (), "plan")
        return pl.pallas_call(
            functools.partial(main_kernel, subs, prior),
            out_shape=outs,
            in_specs=[smem] + [vmem_spec()] * 4,
            out_specs=(vmem_spec(),) * 3,
            scratch_shapes=[
                vmem((count + 8, LANES), f32),
                vmem((slots, LANES), f32),
                vmem((owners, slots + META, LANES), bf16),
            ]
            + arrays
            + [dma((owners,)), dma((owners,))]
            + semaphores,
            compiler_params=pltpu.CompilerParams(
                collective_id=1, has_side_effects=True, vmem_limit_bytes=VMEM_BYTES
            ),
            name="main",
        )(source, vectors, meta, old_centroids, old_codebooks)

    fresh, errors, books = lax.cond(flag[0, 0] > 0.0, again, lambda: (fresh, errors, books))
    return fresh, errors.reshape(owned), books


def solution(mesh):
    in_specs = (
        P("rows", "dims"),
        P("rows"),
        P("rows", "dims"),
        P("rows", "dims"),
        P("rows", "dims"),
    )
    out_specs = (P("rows", "dims"), P("rows"), P("rows", "dims"))
    return jax.shard_map(body, mesh=mesh, in_specs=in_specs, out_specs=out_specs, check_vma=False)
```

time: 167 us -> 146 us (0.87)
  Pallas kernels: 163 us -> 141 us
    pallas_call x2, Pallas kernels: 163 us -> 141 us  [the longest x1 134 us: body(): pl.pallas_call(functools.partial(fast_kernel, subs, prior), out_shape=out...]
where the time goes in v3:
time: 146 us; the launch traced here: 145 us
  Pallas kernels  141 us (97%)
  local copies, waits for them, and re-layouts  3.27 us (2%)
    pallas_call x1, Pallas kernels, body(): pl.pallas_call(functools.partial(fast_kernel, subs, prior), out_shape=out...  134 us
    pallas_call x1, Pallas kernels, plan(): pl.pallas_call(functools.partial(kernel, owned), out_shape=shapes, in_spe...  7.04 us
    unnamed x15, local copies, waits for them, and re-layouts  3.27 us

profile of v3, /device:TPU:6, one launch (start us, length us, event | category | flops | bytes accessed | tf_op | source)
XLA Modules:
  0.0 145.4 jit_solution(7250435758818529430)
XLA Ops:
  0.6 0.0 copy-start
  0.6 7.0 %split_plan.1 = (bf16[64,16,128]{2,1,0:T(8,128)(2,1)}, s32[64,128]{1,0:T(8,128)}, bf16[32,128]{1,0:T(8,128)(2,1)}, s32[1,256]{1,0:T(1,128)}) custom-call(s32[1,4096]{1,0:T(1,128)} %bitcast.7, s32[8,4096]{1,0:T(8,128)} %bitcast.5), custom_call_target="tpu_custom_call" | custom-call | tf_op jit(solution)/shard_map/split_plan/pallas_call | solution.py:771
  7.7 0.0 copy-start.1
  7.7 0.0 copy-start.2
  7.7 0.0 copy-start.3
  7.7 134.3 %fast.1 = (f32[1024,128]{1,0:T(8,128)S(1)}, f32[8,128]{1,0:T(8,128)S(1)}, f32[4,128]{1,0:T(4,128)S(1)}, f32[1,128]{1,0:T(1,128)}) custom-call(s32[64,128]{1,0:T(8,128)} %get-tuple-element.50.from_ref, s32[1,256]{1,0:T(1,128)} %get-tuple-element.51.spill_from_ref, bf16[4096,128]{1,0:T(8,128)(2,1)} %vec_ref.1, ...), custom_call_target="tpu_custom_call" | custom-call | tf_op jit(solution)/shard_map/fast/pallas_call | solution.py:786
  142.0 0.0 copy-start.5
  142.1 0.7 copy-done.5
  142.8 0.0 copy-start.4
  142.8 0.0 copy-done
  142.8 0.0 copy-done.1
  142.8 0.0 copy-done.2
  142.8 0.0 copy-done.3
  142.8 0.6 copy-done.4
  143.4 0.8 copy.17
  144.2 0.6 copy.18
  144.8 0.6 copy.19
  (1 shorter events, 0.0 us)
Async XLA Ops:
  0.6 142.1 %copy-start = (bf16[4096,128]{1,0:T(8,128)(2,1)S(1)}, bf16[4096,128]{1,0:T(8,128)(2,1)}, u32[]{:S(2)}) copy-start(bf16[4096,128]{1,0:T(8,128)(2,1)} %vec_ref.1) | copy-start | bytes 3145732
  7.7 135.1 %copy-start.1 = (f32[1024,128]{1,0:T(8,128)S(1)}, f32[1024,128]{1,0:T(8,128)}, u32[]{:S(2)}) copy-start(f32[1024,128]{1,0:T(8,128)} %old_ref.1) | copy-start | bytes 1572868
  7.7 135.1 %copy-start.2 = (s32[4096,8]{0,1:T(8,128)S(1)}, s32[4096,8]{0,1:T(8,128)}, u32[]{:S(2)}) copy-start(s32[4096,8]{0,1:T(8,128)} %param.9) | copy-start | bytes 393220
  7.7 135.1 %copy-start.3 = (s32[4096]{0:T(1024)S(1)}, s32[4096]{0:T(1024)}, u32[]{:S(2)}) copy-start(s32[4096]{0:T(1024)} %param.8) | copy-start | bytes 49156
  142.0 0.7 copy-start.5
  142.8 0.7 copy-start.4

commit v4 on v3

--- a/solution.py
+++ b/solution.py
@@ -117,19 +117,18 @@
     lower_index = (index & 63).astype(jnp.float32)
     words = (codes_ref[...] + 1).astype(jnp.float32)
 
-    def spread(row):
-        return dot(jnp.where(mine, row, 0.0).astype(jnp.bfloat16), placed, NT)
-
-    for m in range(subs):
-        wide[:, m, :] = spread(words[m : m + 1, :])
-    seen = spread(value)
-    wide[:, subs, :] = seen
+    values = [words[m : m + 1, :] for m in range(subs)] + [value, upper_index, lower_index]
+    given = jnp.concatenate([jnp.where(mine, row, 0.0).astype(jnp.bfloat16) for row in values], axis=0)
+    given = dot(given, placed, NT)
+    given = [given[m * owners : (m + 1) * owners, :] for m in range(len(values))]
+    for m in range(subs + 1):
+        wide[:, m, :] = given[m]
     wide[:, subs + 1, :] = start
     wide[:, subs + 2, :] = start + beyond
     wide[:, subs + 3, :] = jnp.broadcast_to(jnp.where(total > SPILL, 1.0, 0.0), (owners, LANES))
     for m in range(subs + 4, META):
         wide[:, m, :] = jnp.zeros((owners, slots), jnp.float32)
-    high, low = spread(upper_index), spread(lower_index)
+    seen, high, low = given[subs:]
     from_ref[...] = jnp.where(seen > 0.0, high * 64.0 + low, float(count)).astype(jnp.int32)
     meta_ref[...] = wide[...].astype(jnp.bfloat16)
     row = lax.broadcasted_iota(jnp.int32, (META - subs, count), 0)
@@ -631,18 +630,19 @@
     land[0, 0:NEAR, :] = tmp[0:NEAR, :].astype(jnp.bfloat16)
     land[0, NEAR:, :] = meta_ref[me]
 
-    @pl.loop(1, ys)
+    ring = 2 * ys
+
+    @pl.loop(1, ys + ring)
     def _(k):
         send_to(k)
 
-    ring = 2 * ys
     pieces = ring // GROUP
 
     @pl.loop(0, steps)
     def _(t):
         @pl.loop(0, ring)
         def _(q):
-            k = ys + t * ring + q
+            k = ys + (t + 1) * ring + q
 
             @pl.when(k < owners)
             def _():
@@ -671,13 +671,13 @@
 
         @pl.loop(0, pieces)
         def _(q):
-            g = (t - 2) * pieces + q + 1
+            g = (t - 1) * pieces + q + 1
 
             @pl.when(g >= 0)
             def _():
                 process(g)
 
-    done = (steps - 2) * pieces + 1
+    done = (steps - 1) * pieces + 1
 
     @pl.loop(max(done, 0), owners // GROUP)
     def _(g):

time: 146 us -> 145 us (level)
    pallas_call x1, Pallas kernels: 7.04 us -> 4.63 us  [plan(): pl.pallas_call(functools.partial(kernel, owned), out_shape=shapes, in_spe...]
where the time goes in v4:
time: 145 us; the launch traced here: 144 us
  Pallas kernels  140 us (97%)
  local copies, waits for them, and re-layouts  3.28 us (2%)
    pallas_call x1, Pallas kernels, body(): pl.pallas_call(functools.partial(fast_kernel, subs, prior), out_shape=out...  136 us
    pallas_call x1, Pallas kernels, plan(): pl.pallas_call(functools.partial(kernel, owned), out_shape=shapes, in_spe...  4.63 us
    unnamed x15, local copies, waits for them, and re-layouts  3.28 us

profile of v4, /device:TPU:6, one launch (start us, length us, event | category | flops | bytes accessed | tf_op | source)
XLA Modules:
  0.0 144.3 jit_solution(15351245069379365969)
XLA Ops:
  0.6 0.0 copy-start
  0.6 4.6 %split_plan.1 = (bf16[64,16,128]{2,1,0:T(8,128)(2,1)}, s32[64,128]{1,0:T(8,128)}, bf16[32,128]{1,0:T(8,128)(2,1)}, s32[1,256]{1,0:T(1,128)}) custom-call(s32[1,4096]{1,0:T(1,128)} %bitcast.7, s32[8,4096]{1,0:T(8,128)} %bitcast.5), custom_call_target="tpu_custom_call" | custom-call | tf_op jit(solution)/shard_map/split_plan/pallas_call | solution.py:771
  5.3 0.0 copy-start.1
  5.3 0.0 copy-start.2
  5.3 0.0 copy-start.3
  5.3 135.7 %fast.1 = (f32[1024,128]{1,0:T(8,128)S(1)}, f32[8,128]{1,0:T(8,128)S(1)}, f32[4,128]{1,0:T(4,128)S(1)}, f32[1,128]{1,0:T(1,128)}) custom-call(s32[64,128]{1,0:T(8,128)} %get-tuple-element.50.from_ref, s32[1,256]{1,0:T(1,128)} %get-tuple-element.51.spill_from_ref, bf16[4096,128]{1,0:T(8,128)(2,1)} %vec_ref.1, ...), custom_call_target="tpu_custom_call" | custom-call | tf_op jit(solution)/shard_map/fast/pallas_call | solution.py:786
  141.0 0.0 copy-start.5
  141.0 0.7 copy-done.5
  141.7 0.0 copy-start.4
  141.7 0.0 copy-done
  141.7 0.0 copy-done.1
  141.7 0.0 copy-done.2
  141.7 0.0 copy-done.3
  141.7 0.6 copy-done.4
  142.4 0.8 copy.17
  143.1 0.6 copy.18
  143.7 0.6 copy.19
  (1 shorter events, 0.0 us)
Async XLA Ops:
  0.6 141.1 %copy-start = (bf16[4096,128]{1,0:T(8,128)(2,1)S(1)}, bf16[4096,128]{1,0:T(8,128)(2,1)}, u32[]{:S(2)}) copy-start(bf16[4096,128]{1,0:T(8,128)(2,1)} %vec_ref.1) | copy-start | bytes 3145732
  5.3 136.4 %copy-start.1 = (f32[1024,128]{1,0:T(8,128)S(1)}, f32[1024,128]{1,0:T(8,128)}, u32[]{:S(2)}) copy-start(f32[1024,128]{1,0:T(8,128)} %old_ref.1) | copy-start | bytes 1572868
  5.3 136.4 %copy-start.2 = (s32[4096,8]{0,1:T(8,128)S(1)}, s32[4096,8]{0,1:T(8,128)}, u32[]{:S(2)}) copy-start(s32[4096,8]{0,1:T(8,128)} %param.9) | copy-start | bytes 393220
  5.3 136.4 %copy-start.3 = (s32[4096]{0:T(1024)S(1)}, s32[4096]{0:T(1024)}, u32[]{:S(2)}) copy-start(s32[4096]{0:T(1024)} %param.8) | copy-start | bytes 49156
  141.0 0.7 copy-start.5
  141.7 0.7 copy-start.4
